TPU v7x, 32 devices: a whole 2x2x4 slice. The times are simulated.
32 devices in a mesh: gx: 4 (over z), gy: 4 (over x, core), gz: 2 (over y).
Axes of the slice: x: 2, y: 2, z: 4, core: 2. Of those that a mesh axis runs over, the one named last changes fastest.
Arguments:
- conductivity: float32 [16, 64, 512], P('gx', 'gz', 'gy'), may hold values from 0.2 to 5
- initial_guess: float32 [16, 64, 512], P('gx', 'gz', 'gy'), may hold values from -6 to 6
- right_side: float32 [16, 64, 512], P('gx', 'gz', 'gy')
Outputs:
- fine_solution: float32 [16, 64, 512], P('gx', 'gz', 'gy')
- level_one_solution: float32 [8, 32, 256], P('gx', 'gz', 'gy')
- level_two_solution: float32 [4, 16, 128], P(None, 'gz', 'gy')
- level_three_solution: float32 [2, 8, 64], P(None, 'gz', 'gy')
- level_three_residual: float32 [2, 8, 64], P(None, 'gz', 'gy')
All inputs are finite; a program needn't handle non-finite values.
Results may differ from a plain program's by a relative error of at most 0.000034.
Values sent between devices are 32-bit elements; how exact they have to be, the bound alone decides.
A program may use at most 64 MiB of HBM per device.

v0:
```python
import jax
import jax.numpy as jnp
from jax import lax
from jax.sharding import PartitionSpec as P

SWEEPS = 3


lower_bound = 0.25
upper_bound = 2.0


def with_halo(block, sides, width):
    for axis, dim in sides:
        count = lax.axis_size(axis)
        forward = [(i, i + 1) for i in range(count - 1)]
        backward = [(target, source) for source, target in forward]
        low = lax.ppermute(
            lax.slice_in_dim(block, block.shape[dim] - width, None, axis=dim), axis, forward
        )
        high = lax.ppermute(lax.slice_in_dim(block, 0, width, axis=dim), axis, backward)
        block = jnp.concatenate([low, block, high], axis=dim)
    return block


def extend(bundle):
    return with_halo(bundle, (("gx", 1), ("gy", 3), ("gz", 2)), 1)


def deep_extend(bundle, merged):
    if merged:
        grown = with_halo(bundle, (("gy", 3), ("gz", 2)), 4)
        return jnp.pad(grown, ((0, 0), (4, 4), (0, 0), (0, 0)))
    return with_halo(bundle, (("gx", 1), ("gy", 3), ("gz", 2)), 4)


def neighbours(padded):
    return [
        padded[:-2, 1:-1, 1:-1],
        padded[2:, 1:-1, 1:-1],
        padded[1:-1, :-2, 1:-1],
        padded[1:-1, 2:, 1:-1],
        padded[1:-1, 1:-1, :-2],
        padded[1:-1, 1:-1, 2:],
    ]


def face_terms(conduct):
    others = neighbours(extend(conduct[None])[0])
    weights = [0.5 * (conduct + other) for other in others]
    diagonal = weights[0] + weights[1] + weights[2] + weights[3] + weights[4] + weights[5]
    return (weights, diagonal)


def operate(field, weights, diagonal):
    others = neighbours(extend(field[None])[0])
    result = diagonal * field
    for face_index in range(6):
        result = result - weights[face_index] * others[face_index]
    return result


def smooth(source, conduct):
    theta = 0.5 * (upper_bound + lower_bound)
    delta = 0.5 * (upper_bound - lower_bound)
    sigma = theta / delta
    weights, diagonal = face_terms(conduct)
    solution = jnp.zeros_like(source)
    residual = source
    direction = residual / (theta * diagonal)
    ratio_now = 1.0 / sigma
    for sweep_index in range(SWEEPS):
        solution = solution + direction
        residual = residual - operate(direction, weights, diagonal)
        if sweep_index + 1 < SWEEPS:
            ratio_next = 1.0 / (2.0 * sigma - ratio_now)
            direction = (
                ratio_next * ratio_now * direction + 2.0 * ratio_next / delta * residual / diagonal
            )
            ratio_now = ratio_next
    return (solution, residual)


def local_operate(field, weights, diagonal):
    others = neighbours(jnp.pad(field, 1))
    result = diagonal * field
    for face_index in range(6):
        result = result - weights[face_index] * others[face_index]
    return result


def smooth_deep(source, start, conduct, merged):
    theta = 0.5 * (upper_bound + lower_bound)
    delta = 0.5 * (upper_bound - lower_bound)
    sigma = theta / delta
    members = [conduct, source, jnp.ones_like(source)]
    if start is not None:
        members.append(start)
    grown = deep_extend(jnp.stack(members), merged)
    padded_conduct = grown[0]
    padded_source = grown[1]
    inside = grown[2]
    others = neighbours(jnp.pad(padded_conduct, 1))
    weights = [0.5 * (padded_conduct + other) for other in others]
    diagonal = weights[0] + weights[1] + weights[2] + weights[3] + weights[4] + weights[5]
    safe_diagonal = jnp.where(inside > 0.5, diagonal, 1.0)
    if start is None:
        solution = jnp.zeros_like(padded_source)
        residual = padded_source
    else:
        solution = grown[3]
        residual = padded_source - local_operate(solution, weights, diagonal)
    direction = inside * (residual / (theta * safe_diagonal))
    ratio_now = 1.0 / sigma
    for sweep_index in range(SWEEPS):
        solution = solution + direction
        residual = residual - local_operate(direction, weights, diagonal)
        if sweep_index + 1 < SWEEPS:
            ratio_next = 1.0 / (2.0 * sigma - ratio_now)
            direction = inside * (
                ratio_next * ratio_now * direction
                + 2.0 * ratio_next / delta * residual / safe_diagonal
            )
            ratio_now = ratio_next
    return (solution[4:-4, 4:-4, 4:-4], residual[4:-4, 4:-4, 4:-4])


def level_smooth(source, start, conduct, merged):
    extents = source.shape[1:] if merged else source.shape
    if min(extents) >= 4:
        return smooth_deep(source, start, conduct, merged)
    return smooth(source, conduct)


def coarse_sum(field):
    first, second, third = field.shape
    blocks = field.reshape(first // 2, 2, second // 2, 2, third // 2, 2)
    return jnp.sum(blocks, axis=(1, 3, 5))


def shards(conductivity, initial_guess, right_side):
    fine_solution, residual_zero = level_smooth(right_side, initial_guess, conductivity, False)
    conduct_one = 0.125 * coarse_sum(conductivity)
    level_one_solution, residual_one = level_smooth(
        0.25 * coarse_sum(residual_zero), None, conduct_one, False
    )
    conduct_two = 0.125 * coarse_sum(conduct_one)
    source_two = 0.25 * coarse_sum(residual_one)
    bundle = jnp.stack([source_two, conduct_two])
    bundle = lax.all_gather(bundle, "gx", axis=1, tiled=True)
    level_two_solution, residual_two = level_smooth(bundle[0], None, bundle[1], True)
    conduct_three = 0.125 * coarse_sum(bundle[1])
    level_three_solution, level_three_residual = level_smooth(
        0.25 * coarse_sum(residual_two), None, conduct_three, True
    )
    return (
        fine_solution,
        level_one_solution,
        level_two_solution,
        level_three_solution,
        level_three_residual,
    )


def solution(mesh):
    placed = (P("gx", "gz", "gy"), P("gx", "gz", "gy"), P("gx", "gz", "gy"))
    return jax.shard_map(
        shards,
        mesh=mesh,
        in_specs=placed,
        out_specs=(
            P("gx", "gz", "gy"),
            P("gx", "gz", "gy"),
            P(None, "gz", "gy"),
            P(None, "gz", "gy"),
            P(None, "gz", "gy"),
        ),
        check_vma=False,
    )
```

profile of v0, /device:TPU:14, one launch (start us, length us, event | category | flops | bytes accessed | tf_op | source)
XLA Modules:
  0.0 176.7 jit_solution(10855870154186432490)
XLA Ops:
  0.6 6.3 %reshape.78 = f32[2,2,16,2,64,2]{5,4,3,2,1,0:T(8,128)} reshape(f32[4,32,128]{2,1,0:T(8,128)} %param.3) | data formatting | bytes 131072 | tf_op jit(solution)/shard_map/reshape | solution.py:137
  6.9 2.6 %reduce_sum.69 = f32[2,16,64]{2,1,0:T(8,128)S(1)} reduce(f32[2,2,16,2,64,2]{5,4,3,2,1,0:T(8,128)} %reshape.78, f32[]{:T(128)} %constant.11.clone.1), dimensions={1,3,5}, to_apply=%region_1.2 | reduce | flops 14336 | bytes 73732 | tf_op jit(solution)/shard_map/reduce_sum | solution.py:138
  9.5 2.4 %collective-permute-start.7 = (f32[1,1,16,64]{3,2,1,0:T(8,128)S(1)}, f32[1,1,16,64]{3,2,1,0:T(8,128)S(1)}, u32[]{:S(2)}, u32[]{:S(2)}) collective-permute-start(f32[1,1,16,64]{3,2,1,0:T(8,128)S(1)} %get-tuple-element.115), channel_id=1, source_target_pairs={{8,0},{16,8},{24,16},{9,1},{17,9},{25,17},{10,2},{18,10},{26,18},{... | collective-permute-start | bytes 12296 | tf_op jit(solution)/shard_map/ppermute | solution.py:21
  11.9 3.5 %collective-permute-start.6 = (f32[1,1,16,64]{3,2,1,0:T(8,128)S(1)}, f32[1,1,16,64]{3,2,1,0:T(8,128)S(1)}, u32[]{:S(2)}, u32[]{:S(2)}) collective-permute-start(f32[1,1,16,64]{3,2,1,0:T(8,128)S(1)} %get-tuple-element.114), channel_id=1, source_target_pairs={{0,8},{8,16},{16,24},{1,9},{9,17},{17,25},{2,10},{10,18},{18,26},{... | collective-permute-start | bytes 12296 | tf_op jit(solution)/shard_map/ppermute | solution.py:18
  15.5 2.4 %collective-permute-start.1 = (f32[4,4,32,128]{3,2,1,0:T(8,128)S(1)}, f32[4,4,32,128]{3,2,1,0:T(8,128)S(1)}, u32[]{:S(2)}, u32[]{:S(2)}) collective-permute-start(f32[4,4,32,128]{3,2,1,0:T(8,128)S(1)} %pad_maximum_fusion.3), channel_id=1, source_target_pairs={{8,0},{16,8},{24,16},{9,1},{17,9},{25,17},{10,2},{18,10},{26,18},{... | collective-permute-start | bytes 786440 | tf_op jit(solution)/shard_map/ppermute | solution.py:21
  17.8 3.5 %collective-permute-start = (f32[4,4,32,128]{3,2,1,0:T(8,128)S(1)}, f32[4,4,32,128]{3,2,1,0:T(8,128)S(1)}, u32[]{:S(2)}, u32[]{:S(2)}) collective-permute-start(f32[4,4,32,128]{3,2,1,0:T(8,128)S(1)} %pad_maximum_fusion.3), channel_id=1, source_target_pairs={{0,8},{8,16},{16,24},{1,9},{9,17},{17,25},{2,10},{10,18},{18,26},{... | collective-permute-start | bytes 786440 | tf_op jit(solution)/shard_map/ppermute | solution.py:18
  21.4 1.9 %collective-permute-start.9 = (f32[1,4,16,1]{3,2,1,0:T(8,128)S(1)}, f32[1,4,16,1]{3,2,1,0:T(8,128)S(1)}, u32[]{:S(2)}, u32[]{:S(2)}) collective-permute-start(f32[1,4,16,1]{3,2,1,0:T(8,128)S(1)} %get-tuple-element.106), channel_id=1, source_target_pairs={{2,0},{4,2},{6,4},{3,1},{5,3},{7,5},{10,8},{12,10},{14,12},{11,9},... | collective-permute-start | bytes 776 | tf_op jit(solution)/shard_map/ppermute | solution.py:21
  23.4 2.4 %collective-permute-start.8 = (f32[1,4,16,1]{3,2,1,0:T(8,128)S(1)}, f32[1,4,16,1]{3,2,1,0:T(8,128)S(1)}, u32[]{:S(2)}, u32[]{:S(2)}) collective-permute-start(f32[1,4,16,1]{3,2,1,0:T(8,128)S(1)} %get-tuple-element.105), channel_id=1, source_target_pairs={{0,2},{2,4},{4,6},{1,3},{3,5},{5,7},{8,10},{10,12},{12,14},{9,11},... | collective-permute-start | bytes 776 | tf_op jit(solution)/shard_map/ppermute | solution.py:18
  27.7 2.0 %collective-permute-start.3 = (f32[4,12,32,4]{2,3,1,0:T(4,128)S(1)}, f32[4,12,32,4]{2,3,1,0:T(4,128)S(1)}, u32[]{:S(2)}, u32[]{:S(2)}) collective-permute-start(f32[4,12,32,4]{2,3,1,0:T(4,128)S(1)} %copy.18), channel_id=1, source_target_pairs={{2,0},{4,2},{6,4},{3,1},{5,3},{7,5},{10,8},{12,10},{14,12},{11,9},... | collective-permute-start | bytes 73736 | tf_op jit(solution)/shard_map/ppermute | solution.py:21
  30.0 2.3 %collective-permute-start.2 = (f32[4,12,32,4]{2,3,1,0:T(4,128)S(1)}, f32[4,12,32,4]{2,3,1,0:T(4,128)S(1)}, u32[]{:S(2)}, u32[]{:S(2)}) collective-permute-start(f32[4,12,32,4]{2,3,1,0:T(4,128)S(1)} %copy.17), channel_id=1, source_target_pairs={{0,2},{2,4},{4,6},{1,3},{3,5},{5,7},{8,10},{10,12},{12,14},{9,11},... | collective-permute-start | bytes 73736 | tf_op jit(solution)/shard_map/ppermute | solution.py:18
  32.5 2.4 %collective-permute-start.11 = (f32[1,4,1,66]{3,2,1,0:T(1,128)S(1)}, f32[1,4,1,66]{3,2,1,0:T(1,128)S(1)}, u32[]{:S(2)}, u32[]{:S(2)}) collective-permute-start(f32[1,4,1,66]{3,2,1,0:T(1,128)S(1)} %get-tuple-element.84), channel_id=1, source_target_pairs={{1,0},{3,2},{5,4},{7,6},{9,8},{11,10},{13,12},{15,14},{17,16},{19,... | collective-permute-start | bytes 3176 | tf_op jit(solution)/shard_map/ppermute | solution.py:21
  37.7 4.6 %collective-permute-start.5 = (f32[4,12,4,136]{3,2,1,0:T(4,128)S(1)}, f32[4,12,4,136]{3,2,1,0:T(4,128)S(1)}, u32[]{:S(2)}, u32[]{:S(2)}) collective-permute-start(f32[4,12,4,136]{3,2,1,0:T(4,128)S(1)} %get-tuple-element.62), channel_id=1, source_target_pairs={{1,0},{3,2},{5,4},{7,6},{9,8},{11,10},{13,12},{15,14},{17,16},{19,... | collective-permute-start | bytes 313352 | tf_op jit(solution)/shard_map/ppermute | solution.py:21
  43.7 1.7 collective-permute-done.5
  45.4 4.4 %collective-permute-done.4 = f32[4,12,4,136]{3,2,1,0:T(4,128)S(1)} collective-permute-done((f32[4,12,4,136]{3,2,1,0:T(4,128)S(1)}, f32[4,12,4,136]{3,2,1,0:T(4,128)S(1)}, u32[]{:S(2)}, u32[]{:S(2)}) %collective-permute-start.4) | collective-permute-done | bytes 104480 | tf_op jit(solution)/shard_map/ppermute | solution.py:18
  53.9 5.6 %reshape.77 = f32[2,2,16,2,64,2]{5,4,3,2,1,0:T(8,128)} reshape(f32[4,32,128]{2,1,0:T(8,128)S(1)} %slice_subtract_fusion) | data formatting | bytes 131072 | tf_op jit(solution)/shard_map/reshape | solution.py:137
  59.5 2.5 %reduce_sum.68 = f32[2,16,64]{2,1,0:T(8,128)S(1)} reduce(f32[2,2,16,2,64,2]{5,4,3,2,1,0:T(8,128)} %reshape.77, f32[]{:T(128)} %constant.11.clone.1), dimensions={1,3,5}, to_apply=%region_0.1 | reduce | flops 14336 | bytes 73732 | tf_op jit(solution)/shard_map/reduce_sum | solution.py:138
  62.1 2.0 %collective-permute-start.13 = (f32[1,1,16,64]{3,2,1,0:T(8,128)S(1)}, f32[1,1,16,64]{3,2,1,0:T(8,128)S(1)}, u32[]{:S(2)}, u32[]{:S(2)}) collective-permute-start(f32[1,1,16,64]{3,2,1,0:T(8,128)S(1)} %get-tuple-element.113), channel_id=1, source_target_pairs={{8,0},{16,8},{24,16},{9,1},{17,9},{25,17},{10,2},{18,10},{26,18},{... | collective-permute-start | bytes 12296 | tf_op jit(solution)/shard_map/ppermute | solution.py:21
  64.1 3.9 %collective-permute-start.12 = (f32[1,1,16,64]{3,2,1,0:T(8,128)S(1)}, f32[1,1,16,64]{3,2,1,0:T(8,128)S(1)}, u32[]{:S(2)}, u32[]{:S(2)}) collective-permute-start(f32[1,1,16,64]{3,2,1,0:T(8,128)S(1)} %get-tuple-element.112), channel_id=1, source_target_pairs={{0,8},{8,16},{16,24},{1,9},{9,17},{17,25},{2,10},{10,18},{18,26},{... | collective-permute-start | bytes 12296 | tf_op jit(solution)/shard_map/ppermute | solution.py:18
  68.0 1.7 collective-permute-done.12
  69.8 2.5 %collective-permute-start.15 = (f32[1,4,16,1]{3,2,1,0:T(8,128)S(1)}, f32[1,4,16,1]{3,2,1,0:T(8,128)S(1)}, u32[]{:S(2)}, u32[]{:S(2)}) collective-permute-start(f32[1,4,16,1]{3,2,1,0:T(8,128)S(1)} %get-tuple-element.104), channel_id=1, source_target_pairs={{2,0},{4,2},{6,4},{3,1},{5,3},{7,5},{10,8},{12,10},{14,12},{11,9},... | collective-permute-start | bytes 776 | tf_op jit(solution)/shard_map/ppermute | solution.py:21
  72.3 1.9 %collective-permute-start.14 = (f32[1,4,16,1]{3,2,1,0:T(8,128)S(1)}, f32[1,4,16,1]{3,2,1,0:T(8,128)S(1)}, u32[]{:S(2)}, u32[]{:S(2)}) collective-permute-start(f32[1,4,16,1]{3,2,1,0:T(8,128)S(1)} %get-tuple-element.103), channel_id=1, source_target_pairs={{0,2},{2,4},{4,6},{1,3},{3,5},{5,7},{8,10},{10,12},{12,14},{9,11},... | collective-permute-start | bytes 776 | tf_op jit(solution)/shard_map/ppermute | solution.py:18
  74.2 3.5 %collective-permute-done.14 = f32[1,4,16,1]{3,2,1,0:T(8,128)S(1)} collective-permute-done((f32[1,4,16,1]{3,2,1,0:T(8,128)S(1)}, f32[1,4,16,1]{3,2,1,0:T(8,128)S(1)}, u32[]{:S(2)}, u32[]{:S(2)}) %collective-permute-start.14) | collective-permute-done | bytes 288 | tf_op jit(solution)/shard_map/ppermute | solution.py:18
  80.6 4.2 %collective-permute-done.16 = f32[1,4,1,66]{3,2,1,0:T(1,128)S(1)} collective-permute-done((f32[1,4,1,66]{3,2,1,0:T(1,128)S(1)}, f32[1,4,1,66]{3,2,1,0:T(1,128)S(1)}, u32[]{:S(2)}, u32[]{:S(2)}) %collective-permute-start.16) | collective-permute-done | bytes 1088 | tf_op jit(solution)/shard_map/ppermute | solution.py:18
  84.9 1.9 %collective-permute-start.19 = (f32[1,1,16,64]{3,2,1,0:T(8,128)S(1)}, f32[1,1,16,64]{3,2,1,0:T(8,128)S(1)}, u32[]{:S(2)}, u32[]{:S(2)}) collective-permute-start(f32[1,1,16,64]{3,2,1,0:T(8,128)S(1)} %get-tuple-element.111), channel_id=1, source_target_pairs={{8,0},{16,8},{24,16},{9,1},{17,9},{25,17},{10,2},{18,10},{26,18},{... | collective-permute-start | bytes 12296 | tf_op jit(solution)/shard_map/ppermute | solution.py:21
  86.9 3.9 %collective-permute-start.18 = (f32[1,1,16,64]{3,2,1,0:T(8,128)S(1)}, f32[1,1,16,64]{3,2,1,0:T(8,128)S(1)}, u32[]{:S(2)}, u32[]{:S(2)}) collective-permute-start(f32[1,1,16,64]{3,2,1,0:T(8,128)S(1)} %get-tuple-element.110), channel_id=1, source_target_pairs={{0,8},{8,16},{16,24},{1,9},{9,17},{17,25},{2,10},{10,18},{18,26},{... | collective-permute-start | bytes 12296 | tf_op jit(solution)/shard_map/ppermute | solution.py:18
  92.5 1.9 %collective-permute-start.21 = (f32[1,4,16,1]{3,2,1,0:T(8,128)S(1)}, f32[1,4,16,1]{3,2,1,0:T(8,128)S(1)}, u32[]{:S(2)}, u32[]{:S(2)}) collective-permute-start(f32[1,4,16,1]{3,2,1,0:T(8,128)S(1)} %get-tuple-element.102), channel_id=1, source_target_pairs={{2,0},{4,2},{6,4},{3,1},{5,3},{7,5},{10,8},{12,10},{14,12},{11,9},... | collective-permute-start | bytes 776 | tf_op jit(solution)/shard_map/ppermute | solution.py:21
  94.4 2.4 %collective-permute-start.20 = (f32[1,4,16,1]{3,2,1,0:T(8,128)S(1)}, f32[1,4,16,1]{3,2,1,0:T(8,128)S(1)}, u32[]{:S(2)}, u32[]{:S(2)}) collective-permute-start(f32[1,4,16,1]{3,2,1,0:T(8,128)S(1)} %get-tuple-element.101), channel_id=1, source_target_pairs={{0,2},{2,4},{4,6},{1,3},{3,5},{5,7},{8,10},{10,12},{12,14},{9,11},... | collective-permute-start | bytes 776 | tf_op jit(solution)/shard_map/ppermute | solution.py:18
  96.8 2.8 %collective-permute-done.20 = f32[1,4,16,1]{3,2,1,0:T(8,128)S(1)} collective-permute-done((f32[1,4,16,1]{3,2,1,0:T(8,128)S(1)}, f32[1,4,16,1]{3,2,1,0:T(8,128)S(1)}, u32[]{:S(2)}, u32[]{:S(2)}) %collective-permute-start.20) | collective-permute-done | bytes 288 | tf_op jit(solution)/shard_map/ppermute | solution.py:18
  99.7 1.7 collective-permute-start.23
  102.7 4.2 %collective-permute-done.22 = f32[1,4,1,66]{3,2,1,0:T(1,128)S(1)} collective-permute-done((f32[1,4,1,66]{3,2,1,0:T(1,128)S(1)}, f32[1,4,1,66]{3,2,1,0:T(1,128)S(1)}, u32[]{:S(2)}, u32[]{:S(2)}) %collective-permute-start.22) | collective-permute-done | bytes 1088 | tf_op jit(solution)/shard_map/ppermute | solution.py:18
  107.1 1.9 %collective-permute-start.25 = (f32[1,1,16,64]{3,2,1,0:T(8,128)S(1)}, f32[1,1,16,64]{3,2,1,0:T(8,128)S(1)}, u32[]{:S(2)}, u32[]{:S(2)}) collective-permute-start(f32[1,1,16,64]{3,2,1,0:T(8,128)S(1)} %get-tuple-element.108), channel_id=1, source_target_pairs={{8,0},{16,8},{24,16},{9,1},{17,9},{25,17},{10,2},{18,10},{26,18},{... | collective-permute-start | bytes 12296 | tf_op jit(solution)/shard_map/ppermute | solution.py:21
  109.0 3.9 %collective-permute-start.24 = (f32[1,1,16,64]{3,2,1,0:T(8,128)S(1)}, f32[1,1,16,64]{3,2,1,0:T(8,128)S(1)}, u32[]{:S(2)}, u32[]{:S(2)}) collective-permute-start(f32[1,1,16,64]{3,2,1,0:T(8,128)S(1)} %get-tuple-element.107), channel_id=1, source_target_pairs={{0,8},{8,16},{16,24},{1,9},{9,17},{17,25},{2,10},{10,18},{18,26},{... | collective-permute-start | bytes 12296 | tf_op jit(solution)/shard_map/ppermute | solution.py:18
  114.6 1.9 %collective-permute-start.27 = (f32[1,4,16,1]{3,2,1,0:T(8,128)S(1)}, f32[1,4,16,1]{3,2,1,0:T(8,128)S(1)}, u32[]{:S(2)}, u32[]{:S(2)}) collective-permute-start(f32[1,4,16,1]{3,2,1,0:T(8,128)S(1)} %get-tuple-element.100), channel_id=1, source_target_pairs={{2,0},{4,2},{6,4},{3,1},{5,3},{7,5},{10,8},{12,10},{14,12},{11,9},... | collective-permute-start | bytes 776 | tf_op jit(solution)/shard_map/ppermute | solution.py:21
  116.6 2.4 %collective-permute-start.26 = (f32[1,4,16,1]{3,2,1,0:T(8,128)S(1)}, f32[1,4,16,1]{3,2,1,0:T(8,128)S(1)}, u32[]{:S(2)}, u32[]{:S(2)}) collective-permute-start(f32[1,4,16,1]{3,2,1,0:T(8,128)S(1)} %get-tuple-element.99), channel_id=1, source_target_pairs={{0,2},{2,4},{4,6},{1,3},{3,5},{5,7},{8,10},{10,12},{12,14},{9,11},... | collective-permute-start | bytes 776 | tf_op jit(solution)/shard_map/ppermute | solution.py:18
  119.0 2.8 %collective-permute-done.26 = f32[1,4,16,1]{3,2,1,0:T(8,128)S(1)} collective-permute-done((f32[1,4,16,1]{3,2,1,0:T(8,128)S(1)}, f32[1,4,16,1]{3,2,1,0:T(8,128)S(1)}, u32[]{:S(2)}, u32[]{:S(2)}) %collective-permute-start.26) | collective-permute-done | bytes 288 | tf_op jit(solution)/shard_map/ppermute | solution.py:18
  121.9 1.7 collective-permute-start.29
  125.4 3.6 %collective-permute-done.28 = f32[1,4,1,66]{3,2,1,0:T(1,128)S(1)} collective-permute-done((f32[1,4,1,66]{3,2,1,0:T(1,128)S(1)}, f32[1,4,1,66]{3,2,1,0:T(1,128)S(1)}, u32[]{:S(2)}, u32[]{:S(2)}) %collective-permute-start.28) | collective-permute-done | bytes 1088 | tf_op jit(solution)/shard_map/ppermute | solution.py:18
  130.2 14.2 %all_gather.3 = f32[2,4,8,32]{3,2,1,0:T(8,128)S(1)} all-gather(f32[2,1,8,32]{3,2,1,0:T(8,128)S(1)} %pad_maximum_fusion.12), channel_id=1, replica_groups=mesh['gx'=4,'gy'=4,'gz'=2] {'gx'}, dimensions={1}, use_global_device_ids=true | all-gather | bytes 10240 | tf_op jit(solution)/shard_map/all_gather | solution.py:150
  144.5 1.9 %collective-permute-start.31 = (f32[3,4,8,4]{3,2,1,0:T(8,128)S(1)}, f32[3,4,8,4]{3,2,1,0:T(8,128)S(1)}, u32[]{:S(2)}, u32[]{:S(2)}) collective-permute-start(f32[3,4,8,4]{3,2,1,0:T(8,128)S(1)} %get-tuple-element.94), channel_id=1, source_target_pairs={{2,0},{4,2},{6,4},{3,1},{5,3},{7,5},{10,8},{12,10},{14,12},{11,9},... | collective-permute-start | bytes 4616 | tf_op jit(solution)/shard_map/ppermute | solution.py:21
  146.4 2.4 %collective-permute-start.30 = (f32[3,4,8,4]{3,2,1,0:T(8,128)S(1)}, f32[3,4,8,4]{3,2,1,0:T(8,128)S(1)}, u32[]{:S(2)}, u32[]{:S(2)}) collective-permute-start(f32[3,4,8,4]{3,2,1,0:T(8,128)S(1)} %get-tuple-element.93), channel_id=1, source_target_pairs={{0,2},{2,4},{4,6},{1,3},{3,5},{5,7},{8,10},{10,12},{12,14},{9,11},... | collective-permute-start | bytes 4616 | tf_op jit(solution)/shard_map/ppermute | solution.py:18
  149.1 2.7 %collective-permute-done.30 = f32[3,4,8,4]{3,2,1,0:T(8,128)S(1)} collective-permute-done((f32[3,4,8,4]{3,2,1,0:T(8,128)S(1)}, f32[3,4,8,4]{3,2,1,0:T(8,128)S(1)}, u32[]{:S(2)}, u32[]{:S(2)}) %collective-permute-start.30) | collective-permute-done | bytes 1568 | tf_op jit(solution)/shard_map/ppermute | solution.py:18
  151.9 1.7 collective-permute-start.33
  155.1 4.2 %collective-permute-done.32 = f32[3,4,4,40]{3,2,1,0:T(4,128)S(1)} collective-permute-done((f32[3,4,4,40]{3,2,1,0:T(4,128)S(1)}, f32[3,4,4,40]{3,2,1,0:T(4,128)S(1)}, u32[]{:S(2)}, u32[]{:S(2)}) %collective-permute-start.32) | collective-permute-done | bytes 7712 | tf_op jit(solution)/shard_map/ppermute | solution.py:18
  160.5 1.9 %collective-permute-start.35 = (f32[3,2,4,4]{3,2,1,0:T(4,128)S(1)}, f32[3,2,4,4]{3,2,1,0:T(4,128)S(1)}, u32[]{:S(2)}, u32[]{:S(2)}) collective-permute-start(f32[3,2,4,4]{3,2,1,0:T(4,128)S(1)} %get-tuple-element.117), channel_id=1, source_target_pairs={{2,0},{4,2},{6,4},{3,1},{5,3},{7,5},{10,8},{12,10},{14,12},{11,9},... | collective-permute-start | bytes 1160 | tf_op jit(solution)/shard_map/ppermute | solution.py:21
  162.4 2.4 %collective-permute-start.34 = (f32[3,2,4,4]{3,2,1,0:T(4,128)S(1)}, f32[3,2,4,4]{3,2,1,0:T(4,128)S(1)}, u32[]{:S(2)}, u32[]{:S(2)}) collective-permute-start(f32[3,2,4,4]{3,2,1,0:T(4,128)S(1)} %get-tuple-element.116), channel_id=1, source_target_pairs={{0,2},{2,4},{4,6},{1,3},{3,5},{5,7},{8,10},{10,12},{12,14},{9,11},... | collective-permute-start | bytes 1160 | tf_op jit(solution)/shard_map/ppermute | solution.py:18
  165.6 1.8 %collective-permute-done.34 = f32[3,2,4,4]{3,2,1,0:T(4,128)S(1)} collective-permute-done((f32[3,2,4,4]{3,2,1,0:T(4,128)S(1)}, f32[3,2,4,4]{3,2,1,0:T(4,128)S(1)}, u32[]{:S(2)}, u32[]{:S(2)}) %collective-permute-start.34) | collective-permute-done | bytes 416 | tf_op jit(solution)/shard_map/ppermute | solution.py:18
  167.5 1.6 collective-permute-start.37
  171.1 3.6 %collective-permute-done.36 = f32[3,2,4,24]{3,2,1,0:T(4,128)S(1)} collective-permute-done((f32[3,2,4,24]{3,2,1,0:T(4,128)S(1)}, f32[3,2,4,24]{3,2,1,0:T(4,128)S(1)}, u32[]{:S(2)}, u32[]{:S(2)}) %collective-permute-start.36) | collective-permute-done | bytes 2336 | tf_op jit(solution)/shard_map/ppermute | solution.py:18
  (120 shorter events, 29.7 us)
Async XLA Ops:
  6.9 8.5 %copy-start = (f32[4,32,128]{2,1,0:T(8,128)S(1)}, f32[4,32,128]{2,1,0:T(8,128)}, u32[]{:S(2)}) copy-start(f32[4,32,128]{2,1,0:T(8,128)} %param.3) | copy-start | bytes 196612
  6.9 8.5 %copy-start.1 = (f32[4,32,128]{2,1,0:T(8,128)S(1)}, f32[4,32,128]{2,1,0:T(8,128)}, u32[]{:S(2)}) copy-start(f32[4,32,128]{2,1,0:T(8,128)} %param.4) | copy-start | bytes 196612
  6.9 8.5 %copy-start.2 = (f32[4,32,128]{2,1,0:T(8,128)S(1)}, f32[4,32,128]{2,1,0:T(8,128)}, u32[]{:S(2)}) copy-start(f32[4,32,128]{2,1,0:T(8,128)} %param.5) | copy-start | bytes 196612
  9.5 11.8 %collective-permute-start.7 = (f32[1,1,16,64]{3,2,1,0:T(8,128)S(1)}, f32[1,1,16,64]{3,2,1,0:T(8,128)S(1)}, u32[]{:S(2)}, u32[]{:S(2)}) collective-permute-start(f32[1,1,16,64]{3,2,1,0:T(8,128)S(1)} %get-tuple-element.115), channel_id=1, source_target_pairs={{8,0},{16,8},{24,16},{9,1},{17,9},{25,17},{10,2},{18,10},{26,18},{... | collective-permute-start | bytes 12296 | tf_op jit(solution)/shard_map/ppermute | solution.py:21
  11.9 9.4 %collective-permute-start.6 = (f32[1,1,16,64]{3,2,1,0:T(8,128)S(1)}, f32[1,1,16,64]{3,2,1,0:T(8,128)S(1)}, u32[]{:S(2)}, u32[]{:S(2)}) collective-permute-start(f32[1,1,16,64]{3,2,1,0:T(8,128)S(1)} %get-tuple-element.114), channel_id=1, source_target_pairs={{0,8},{8,16},{16,24},{1,9},{9,17},{17,25},{2,10},{10,18},{18,26},{... | collective-permute-start | bytes 12296 | tf_op jit(solution)/shard_map/ppermute | solution.py:18
  15.5 10.3 %collective-permute-start.1 = (f32[4,4,32,128]{3,2,1,0:T(8,128)S(1)}, f32[4,4,32,128]{3,2,1,0:T(8,128)S(1)}, u32[]{:S(2)}, u32[]{:S(2)}) collective-permute-start(f32[4,4,32,128]{3,2,1,0:T(8,128)S(1)} %pad_maximum_fusion.3), channel_id=1, source_target_pairs={{8,0},{16,8},{24,16},{9,1},{17,9},{25,17},{10,2},{18,10},{26,18},{... | collective-permute-start | bytes 786440 | tf_op jit(solution)/shard_map/ppermute | solution.py:21
  17.8 9.1 %collective-permute-start = (f32[4,4,32,128]{3,2,1,0:T(8,128)S(1)}, f32[4,4,32,128]{3,2,1,0:T(8,128)S(1)}, u32[]{:S(2)}, u32[]{:S(2)}) collective-permute-start(f32[4,4,32,128]{3,2,1,0:T(8,128)S(1)} %pad_maximum_fusion.3), channel_id=1, source_target_pairs={{0,8},{8,16},{16,24},{1,9},{9,17},{17,25},{2,10},{10,18},{18,26},{... | collective-permute-start | bytes 786440 | tf_op jit(solution)/shard_map/ppermute | solution.py:18
  21.4 10.9 %collective-permute-start.9 = (f32[1,4,16,1]{3,2,1,0:T(8,128)S(1)}, f32[1,4,16,1]{3,2,1,0:T(8,128)S(1)}, u32[]{:S(2)}, u32[]{:S(2)}) collective-permute-start(f32[1,4,16,1]{3,2,1,0:T(8,128)S(1)} %get-tuple-element.106), channel_id=1, source_target_pairs={{2,0},{4,2},{6,4},{3,1},{5,3},{7,5},{10,8},{12,10},{14,12},{11,9},... | collective-permute-start | bytes 776 | tf_op jit(solution)/shard_map/ppermute | solution.py:21
  23.4 9.0 %collective-permute-start.8 = (f32[1,4,16,1]{3,2,1,0:T(8,128)S(1)}, f32[1,4,16,1]{3,2,1,0:T(8,128)S(1)}, u32[]{:S(2)}, u32[]{:S(2)}) collective-permute-start(f32[1,4,16,1]{3,2,1,0:T(8,128)S(1)} %get-tuple-element.105), channel_id=1, source_target_pairs={{0,2},{2,4},{4,6},{1,3},{3,5},{5,7},{8,10},{10,12},{12,14},{9,11},... | collective-permute-start | bytes 776 | tf_op jit(solution)/shard_map/ppermute | solution.py:18
  27.7 8.5 %collective-permute-start.3 = (f32[4,12,32,4]{2,3,1,0:T(4,128)S(1)}, f32[4,12,32,4]{2,3,1,0:T(4,128)S(1)}, u32[]{:S(2)}, u32[]{:S(2)}) collective-permute-start(f32[4,12,32,4]{2,3,1,0:T(4,128)S(1)} %copy.18), channel_id=1, source_target_pairs={{2,0},{4,2},{6,4},{3,1},{5,3},{7,5},{10,8},{12,10},{14,12},{11,9},... | collective-permute-start | bytes 73736 | tf_op jit(solution)/shard_map/ppermute | solution.py:21
  30.0 6.5 %collective-permute-start.2 = (f32[4,12,32,4]{2,3,1,0:T(4,128)S(1)}, f32[4,12,32,4]{2,3,1,0:T(4,128)S(1)}, u32[]{:S(2)}, u32[]{:S(2)}) collective-permute-start(f32[4,12,32,4]{2,3,1,0:T(4,128)S(1)} %copy.17), channel_id=1, source_target_pairs={{0,2},{2,4},{4,6},{1,3},{3,5},{5,7},{8,10},{10,12},{12,14},{9,11},... | collective-permute-start | bytes 73736 | tf_op jit(solution)/shard_map/ppermute | solution.py:18
  32.5 11.1 %collective-permute-start.11 = (f32[1,4,1,66]{3,2,1,0:T(1,128)S(1)}, f32[1,4,1,66]{3,2,1,0:T(1,128)S(1)}, u32[]{:S(2)}, u32[]{:S(2)}) collective-permute-start(f32[1,4,1,66]{3,2,1,0:T(1,128)S(1)} %get-tuple-element.84), channel_id=1, source_target_pairs={{1,0},{3,2},{5,4},{7,6},{9,8},{11,10},{13,12},{15,14},{17,16},{19,... | collective-permute-start | bytes 3176 | tf_op jit(solution)/shard_map/ppermute | solution.py:21
  34.9 8.7 %collective-permute-start.10 = (f32[1,4,1,66]{3,2,1,0:T(1,128)S(1)}, f32[1,4,1,66]{3,2,1,0:T(1,128)S(1)}, u32[]{:S(2)}, u32[]{:S(2)}) collective-permute-start(f32[1,4,1,66]{3,2,1,0:T(1,128)S(1)} %get-tuple-element.83), channel_id=1, source_target_pairs={{0,1},{2,3},{4,5},{6,7},{8,9},{10,11},{12,13},{14,15},{16,17},{18,... | collective-permute-start | bytes 3176 | tf_op jit(solution)/shard_map/ppermute | solution.py:18
  37.7 7.7 %collective-permute-start.5 = (f32[4,12,4,136]{3,2,1,0:T(4,128)S(1)}, f32[4,12,4,136]{3,2,1,0:T(4,128)S(1)}, u32[]{:S(2)}, u32[]{:S(2)}) collective-permute-start(f32[4,12,4,136]{3,2,1,0:T(4,128)S(1)} %get-tuple-element.62), channel_id=1, source_target_pairs={{1,0},{3,2},{5,4},{7,6},{9,8},{11,10},{13,12},{15,14},{17,16},{19,... | collective-permute-start | bytes 313352 | tf_op jit(solution)/shard_map/ppermute | solution.py:21
  42.2 7.6 %collective-permute-start.4 = (f32[4,12,4,136]{3,2,1,0:T(4,128)S(1)}, f32[4,12,4,136]{3,2,1,0:T(4,128)S(1)}, u32[]{:S(2)}, u32[]{:S(2)}) collective-permute-start(f32[4,12,4,136]{3,2,1,0:T(4,128)S(1)} %get-tuple-element.61), channel_id=1, source_target_pairs={{0,1},{2,3},{4,5},{6,7},{8,9},{10,11},{12,13},{14,15},{16,17},{18,... | collective-permute-start | bytes 313352 | tf_op jit(solution)/shard_map/ppermute | solution.py:18
  62.1 5.9 %collective-permute-start.13 = (f32[1,1,16,64]{3,2,1,0:T(8,128)S(1)}, f32[1,1,16,64]{3,2,1,0:T(8,128)S(1)}, u32[]{:S(2)}, u32[]{:S(2)}) collective-permute-start(f32[1,1,16,64]{3,2,1,0:T(8,128)S(1)} %get-tuple-element.113), channel_id=1, source_target_pairs={{8,0},{16,8},{24,16},{9,1},{17,9},{25,17},{10,2},{18,10},{26,18},{... | collective-permute-start | bytes 12296 | tf_op jit(solution)/shard_map/ppermute | solution.py:21
  64.1 5.5 %collective-permute-start.12 = (f32[1,1,16,64]{3,2,1,0:T(8,128)S(1)}, f32[1,1,16,64]{3,2,1,0:T(8,128)S(1)}, u32[]{:S(2)}, u32[]{:S(2)}) collective-permute-start(f32[1,1,16,64]{3,2,1,0:T(8,128)S(1)} %get-tuple-element.112), channel_id=1, source_target_pairs={{0,8},{8,16},{16,24},{1,9},{9,17},{17,25},{2,10},{10,18},{18,26},{... | collective-permute-start | bytes 12296 | tf_op jit(solution)/shard_map/ppermute | solution.py:18
  69.8 4.5 %collective-permute-start.15 = (f32[1,4,16,1]{3,2,1,0:T(8,128)S(1)}, f32[1,4,16,1]{3,2,1,0:T(8,128)S(1)}, u32[]{:S(2)}, u32[]{:S(2)}) collective-permute-start(f32[1,4,16,1]{3,2,1,0:T(8,128)S(1)} %get-tuple-element.104), channel_id=1, source_target_pairs={{2,0},{4,2},{6,4},{3,1},{5,3},{7,5},{10,8},{12,10},{14,12},{11,9},... | collective-permute-start | bytes 776 | tf_op jit(solution)/shard_map/ppermute | solution.py:21
  72.3 5.4 %collective-permute-start.14 = (f32[1,4,16,1]{3,2,1,0:T(8,128)S(1)}, f32[1,4,16,1]{3,2,1,0:T(8,128)S(1)}, u32[]{:S(2)}, u32[]{:S(2)}) collective-permute-start(f32[1,4,16,1]{3,2,1,0:T(8,128)S(1)} %get-tuple-element.103), channel_id=1, source_target_pairs={{0,2},{2,4},{4,6},{1,3},{3,5},{5,7},{8,10},{10,12},{12,14},{9,11},... | collective-permute-start | bytes 776 | tf_op jit(solution)/shard_map/ppermute | solution.py:18
  77.8 2.8 %collective-permute-start.17 = (f32[1,4,1,66]{3,2,1,0:T(1,128)S(1)}, f32[1,4,1,66]{3,2,1,0:T(1,128)S(1)}, u32[]{:S(2)}, u32[]{:S(2)}) collective-permute-start(f32[1,4,1,66]{3,2,1,0:T(1,128)S(1)} %get-tuple-element.82), channel_id=1, source_target_pairs={{1,0},{3,2},{5,4},{7,6},{9,8},{11,10},{13,12},{15,14},{17,16},{19,... | collective-permute-start | bytes 3176 | tf_op jit(solution)/shard_map/ppermute | solution.py:21
  79.2 5.5 %collective-permute-start.16 = (f32[1,4,1,66]{3,2,1,0:T(1,128)S(1)}, f32[1,4,1,66]{3,2,1,0:T(1,128)S(1)}, u32[]{:S(2)}, u32[]{:S(2)}) collective-permute-start(f32[1,4,1,66]{3,2,1,0:T(1,128)S(1)} %get-tuple-element.81), channel_id=1, source_target_pairs={{0,1},{2,3},{4,5},{6,7},{8,9},{10,11},{12,13},{14,15},{16,17},{18,... | collective-permute-start | bytes 3176 | tf_op jit(solution)/shard_map/ppermute | solution.py:18
  84.9 5.9 %collective-permute-start.19 = (f32[1,1,16,64]{3,2,1,0:T(8,128)S(1)}, f32[1,1,16,64]{3,2,1,0:T(8,128)S(1)}, u32[]{:S(2)}, u32[]{:S(2)}) collective-permute-start(f32[1,1,16,64]{3,2,1,0:T(8,128)S(1)} %get-tuple-element.111), channel_id=1, source_target_pairs={{8,0},{16,8},{24,16},{9,1},{17,9},{25,17},{10,2},{18,10},{26,18},{... | collective-permute-start | bytes 12296 | tf_op jit(solution)/shard_map/ppermute | solution.py:21
  86.9 5.5 %collective-permute-start.18 = (f32[1,1,16,64]{3,2,1,0:T(8,128)S(1)}, f32[1,1,16,64]{3,2,1,0:T(8,128)S(1)}, u32[]{:S(2)}, u32[]{:S(2)}) collective-permute-start(f32[1,1,16,64]{3,2,1,0:T(8,128)S(1)} %get-tuple-element.110), channel_id=1, source_target_pairs={{0,8},{8,16},{16,24},{1,9},{9,17},{17,25},{2,10},{10,18},{18,26},{... | collective-permute-start | bytes 12296 | tf_op jit(solution)/shard_map/ppermute | solution.py:18
  92.5 4.3 %collective-permute-start.21 = (f32[1,4,16,1]{3,2,1,0:T(8,128)S(1)}, f32[1,4,16,1]{3,2,1,0:T(8,128)S(1)}, u32[]{:S(2)}, u32[]{:S(2)}) collective-permute-start(f32[1,4,16,1]{3,2,1,0:T(8,128)S(1)} %get-tuple-element.102), channel_id=1, source_target_pairs={{2,0},{4,2},{6,4},{3,1},{5,3},{7,5},{10,8},{12,10},{14,12},{11,9},... | collective-permute-start | bytes 776 | tf_op jit(solution)/shard_map/ppermute | solution.py:21
  94.4 5.2 %collective-permute-start.20 = (f32[1,4,16,1]{3,2,1,0:T(8,128)S(1)}, f32[1,4,16,1]{3,2,1,0:T(8,128)S(1)}, u32[]{:S(2)}, u32[]{:S(2)}) collective-permute-start(f32[1,4,16,1]{3,2,1,0:T(8,128)S(1)} %get-tuple-element.101), channel_id=1, source_target_pairs={{0,2},{2,4},{4,6},{1,3},{3,5},{5,7},{8,10},{10,12},{12,14},{9,11},... | collective-permute-start | bytes 776 | tf_op jit(solution)/shard_map/ppermute | solution.py:18
  99.7 3.0 %collective-permute-start.23 = (f32[1,4,1,66]{3,2,1,0:T(1,128)S(1)}, f32[1,4,1,66]{3,2,1,0:T(1,128)S(1)}, u32[]{:S(2)}, u32[]{:S(2)}) collective-permute-start(f32[1,4,1,66]{3,2,1,0:T(1,128)S(1)} %get-tuple-element.80), channel_id=1, source_target_pairs={{1,0},{3,2},{5,4},{7,6},{9,8},{11,10},{13,12},{15,14},{17,16},{19,... | collective-permute-start | bytes 3176 | tf_op jit(solution)/shard_map/ppermute | solution.py:21
  101.4 5.5 %collective-permute-start.22 = (f32[1,4,1,66]{3,2,1,0:T(1,128)S(1)}, f32[1,4,1,66]{3,2,1,0:T(1,128)S(1)}, u32[]{:S(2)}, u32[]{:S(2)}) collective-permute-start(f32[1,4,1,66]{3,2,1,0:T(1,128)S(1)} %get-tuple-element.79), channel_id=1, source_target_pairs={{0,1},{2,3},{4,5},{6,7},{8,9},{10,11},{12,13},{14,15},{16,17},{18,... | collective-permute-start | bytes 3176 | tf_op jit(solution)/shard_map/ppermute | solution.py:18
  107.1 5.9 %collective-permute-start.25 = (f32[1,1,16,64]{3,2,1,0:T(8,128)S(1)}, f32[1,1,16,64]{3,2,1,0:T(8,128)S(1)}, u32[]{:S(2)}, u32[]{:S(2)}) collective-permute-start(f32[1,1,16,64]{3,2,1,0:T(8,128)S(1)} %get-tuple-element.108), channel_id=1, source_target_pairs={{8,0},{16,8},{24,16},{9,1},{17,9},{25,17},{10,2},{18,10},{26,18},{... | collective-permute-start | bytes 12296 | tf_op jit(solution)/shard_map/ppermute | solution.py:21
  109.0 5.5 %collective-permute-start.24 = (f32[1,1,16,64]{3,2,1,0:T(8,128)S(1)}, f32[1,1,16,64]{3,2,1,0:T(8,128)S(1)}, u32[]{:S(2)}, u32[]{:S(2)}) collective-permute-start(f32[1,1,16,64]{3,2,1,0:T(8,128)S(1)} %get-tuple-element.107), channel_id=1, source_target_pairs={{0,8},{8,16},{16,24},{1,9},{9,17},{17,25},{2,10},{10,18},{18,26},{... | collective-permute-start | bytes 12296 | tf_op jit(solution)/shard_map/ppermute | solution.py:18
  114.6 4.3 %collective-permute-start.27 = (f32[1,4,16,1]{3,2,1,0:T(8,128)S(1)}, f32[1,4,16,1]{3,2,1,0:T(8,128)S(1)}, u32[]{:S(2)}, u32[]{:S(2)}) collective-permute-start(f32[1,4,16,1]{3,2,1,0:T(8,128)S(1)} %get-tuple-element.100), channel_id=1, source_target_pairs={{2,0},{4,2},{6,4},{3,1},{5,3},{7,5},{10,8},{12,10},{14,12},{11,9},... | collective-permute-start | bytes 776 | tf_op jit(solution)/shard_map/ppermute | solution.py:21
  116.6 5.2 %collective-permute-start.26 = (f32[1,4,16,1]{3,2,1,0:T(8,128)S(1)}, f32[1,4,16,1]{3,2,1,0:T(8,128)S(1)}, u32[]{:S(2)}, u32[]{:S(2)}) collective-permute-start(f32[1,4,16,1]{3,2,1,0:T(8,128)S(1)} %get-tuple-element.99), channel_id=1, source_target_pairs={{0,2},{2,4},{4,6},{1,3},{3,5},{5,7},{8,10},{10,12},{12,14},{9,11},... | collective-permute-start | bytes 776 | tf_op jit(solution)/shard_map/ppermute | solution.py:18
  121.9 3.5 %collective-permute-start.29 = (f32[1,4,1,66]{3,2,1,0:T(1,128)S(1)}, f32[1,4,1,66]{3,2,1,0:T(1,128)S(1)}, u32[]{:S(2)}, u32[]{:S(2)}) collective-permute-start(f32[1,4,1,66]{3,2,1,0:T(1,128)S(1)} %get-tuple-element.78), channel_id=1, source_target_pairs={{1,0},{3,2},{5,4},{7,6},{9,8},{11,10},{13,12},{15,14},{17,16},{19,... | collective-permute-start | bytes 3176 | tf_op jit(solution)/shard_map/ppermute | solution.py:21
  123.5 5.5 %collective-permute-start.28 = (f32[1,4,1,66]{3,2,1,0:T(1,128)S(1)}, f32[1,4,1,66]{3,2,1,0:T(1,128)S(1)}, u32[]{:S(2)}, u32[]{:S(2)}) collective-permute-start(f32[1,4,1,66]{3,2,1,0:T(1,128)S(1)} %get-tuple-element.77), channel_id=1, source_target_pairs={{0,1},{2,3},{4,5},{6,7},{8,9},{10,11},{12,13},{14,15},{16,17},{18,... | collective-permute-start | bytes 3176 | tf_op jit(solution)/shard_map/ppermute | solution.py:18
  144.5 4.6 %collective-permute-start.31 = (f32[3,4,8,4]{3,2,1,0:T(8,128)S(1)}, f32[3,4,8,4]{3,2,1,0:T(8,128)S(1)}, u32[]{:S(2)}, u32[]{:S(2)}) collective-permute-start(f32[3,4,8,4]{3,2,1,0:T(8,128)S(1)} %get-tuple-element.94), channel_id=1, source_target_pairs={{2,0},{4,2},{6,4},{3,1},{5,3},{7,5},{10,8},{12,10},{14,12},{11,9},... | collective-permute-start | bytes 4616 | tf_op jit(solution)/shard_map/ppermute | solution.py:21
  146.4 5.4 %collective-permute-start.30 = (f32[3,4,8,4]{3,2,1,0:T(8,128)S(1)}, f32[3,4,8,4]{3,2,1,0:T(8,128)S(1)}, u32[]{:S(2)}, u32[]{:S(2)}) collective-permute-start(f32[3,4,8,4]{3,2,1,0:T(8,128)S(1)} %get-tuple-element.93), channel_id=1, source_target_pairs={{0,2},{2,4},{4,6},{1,3},{3,5},{5,7},{8,10},{10,12},{12,14},{9,11},... | collective-permute-start | bytes 4616 | tf_op jit(solution)/shard_map/ppermute | solution.py:18
  151.9 3.2 %collective-permute-start.33 = (f32[3,4,4,40]{3,2,1,0:T(4,128)S(1)}, f32[3,4,4,40]{3,2,1,0:T(4,128)S(1)}, u32[]{:S(2)}, u32[]{:S(2)}) collective-permute-start(f32[3,4,4,40]{3,2,1,0:T(4,128)S(1)} %get-tuple-element.92), channel_id=1, source_target_pairs={{1,0},{3,2},{5,4},{7,6},{9,8},{11,10},{13,12},{15,14},{17,16},{19,... | collective-permute-start | bytes 23048 | tf_op jit(solution)/shard_map/ppermute | solution.py:21
  153.6 5.7 %collective-permute-start.32 = (f32[3,4,4,40]{3,2,1,0:T(4,128)S(1)}, f32[3,4,4,40]{3,2,1,0:T(4,128)S(1)}, u32[]{:S(2)}, u32[]{:S(2)}) collective-permute-start(f32[3,4,4,40]{3,2,1,0:T(4,128)S(1)} %get-tuple-element.91), channel_id=1, source_target_pairs={{0,1},{2,3},{4,5},{6,7},{8,9},{10,11},{12,13},{14,15},{16,17},{18,... | collective-permute-start | bytes 23048 | tf_op jit(solution)/shard_map/ppermute | solution.py:18
  160.5 5.1 %collective-permute-start.35 = (f32[3,2,4,4]{3,2,1,0:T(4,128)S(1)}, f32[3,2,4,4]{3,2,1,0:T(4,128)S(1)}, u32[]{:S(2)}, u32[]{:S(2)}) collective-permute-start(f32[3,2,4,4]{3,2,1,0:T(4,128)S(1)} %get-tuple-element.117), channel_id=1, source_target_pairs={{2,0},{4,2},{6,4},{3,1},{5,3},{7,5},{10,8},{12,10},{14,12},{11,9},... | collective-permute-start | bytes 1160 | tf_op jit(solution)/shard_map/ppermute | solution.py:21
  162.4 5.0 %collective-permute-start.34 = (f32[3,2,4,4]{3,2,1,0:T(4,128)S(1)}, f32[3,2,4,4]{3,2,1,0:T(4,128)S(1)}, u32[]{:S(2)}, u32[]{:S(2)}) collective-permute-start(f32[3,2,4,4]{3,2,1,0:T(4,128)S(1)} %get-tuple-element.116), channel_id=1, source_target_pairs={{0,2},{2,4},{4,6},{1,3},{3,5},{5,7},{8,10},{10,12},{12,14},{9,11},... | collective-permute-start | bytes 1160 | tf_op jit(solution)/shard_map/ppermute | solution.py:18
  167.5 3.6 %collective-permute-start.37 = (f32[3,2,4,24]{3,2,1,0:T(4,128)S(1)}, f32[3,2,4,24]{3,2,1,0:T(4,128)S(1)}, u32[]{:S(2)}, u32[]{:S(2)}) collective-permute-start(f32[3,2,4,24]{3,2,1,0:T(4,128)S(1)} %pad_maximum_fusion.11), channel_id=1, source_target_pairs={{1,0},{3,2},{5,4},{7,6},{9,8},{11,10},{13,12},{15,14},{17,16},{19,... | collective-permute-start | bytes 6920 | tf_op jit(solution)/shard_map/ppermute | solution.py:21
  169.1 5.6 %collective-permute-start.36 = (f32[3,2,4,24]{3,2,1,0:T(4,128)S(1)}, f32[3,2,4,24]{3,2,1,0:T(4,128)S(1)}, u32[]{:S(2)}, u32[]{:S(2)}) collective-permute-start(f32[3,2,4,24]{3,2,1,0:T(4,128)S(1)} %pad_maximum_fusion.11), channel_id=1, source_target_pairs={{0,1},{2,3},{4,5},{6,7},{8,9},{10,11},{12,13},{14,15},{16,17},{18,... | collective-permute-start | bytes 6920 | tf_op jit(solution)/shard_map/ppermute | solution.py:18
where the time goes:
time: 178 us; the launch traced here: 177 us
  starting transfers between devices  83.8 us (47%)
  waiting for transfers between devices  45.8 us (26%)
  other arithmetic  16.3 us (9%)
  local copies, waits for them, and re-layouts  15.1 us (8%)
  blocking collectives  14.2 us (8%)
    ppermute x19, starting transfers between devices, with_halo(): lax.ppermute(lax.slice_in_dim(block, block.shape[dim] - width, None, axis...  44.1 us
    ppermute x19, waiting for transfers between devices, with_halo(): lax.ppermute(lax.slice_in_dim(block, block.shape[dim] - width, None, axis...  43.8 us
    ppermute x19, starting transfers between devices, with_halo(): lax.ppermute(lax.slice_in_dim(block, 0, width, axis=dim), axis, backward)  39.7 us
    all_gather x1, blocking collectives, shards(): bundle = lax.all_gather(bundle, 'gx', axis=1, tiled=True)  14.2 us
    reshape x3, local copies, waits for them, and re-layouts, coarse_sum(): blocks = field.reshape(first // 2, 2, second // 2, 2, third // 2, 2)  12 us
    reduce_sum x7, other arithmetic, coarse_sum(): return jnp.sum(blocks, axis=(1, 3, 5))  6.18 us
  transfers between devices with their start and end apart: 38, of which 17 were waited for; matrix products, arithmetic and copies ran while one was open for 3% of the time, Pallas kernels for 0%

commit v1 on v0

--- a/solution.py
+++ b/solution.py
@@ -1,6 +1,10 @@
+import functools
+
 import jax
 import jax.numpy as jnp
 from jax import lax
+from jax.experimental import pallas as pl
+from jax.experimental.pallas import tpu as pltpu
 from jax.sharding import PartitionSpec as P
 
 SWEEPS = 3
@@ -162,18 +166,492 @@
     )
 
 
+FIELDS = 3
+WIDTH = 4
+ROWS = 8
+LANES = 128
+
+
+def in_range(index, count):
+    return (index >= 0) & (index < count)
+
+
+def shift(value, amount, axis):
+    return pltpu.roll(value, amount % value.shape[axis], axis)
+
+
+def smooth_planes(conduct, source, start, grown):
+    theta = 0.5 * (upper_bound + lower_bound)
+    delta = 0.5 * (upper_bound - lower_bound)
+    sigma = theta / delta
+    count = len(conduct)
+    edge = 1 if grown else 0
+    weight_x = [None] * (count + 1)
+    for i in range(1, count):
+        weight_x[i] = 0.5 * (conduct[i - 1] + conduct[i])
+    if not grown:
+        weight_x[0] = 0.5 * conduct[0]
+        weight_x[count] = 0.5 * conduct[count - 1]
+    weight_z = [None] * count
+    weight_y = [None] * count
+    inverse = [None] * count
+    for i in range(edge, count - edge):
+        weight_z[i] = 0.5 * (conduct[i] + shift(conduct[i], -1, 0))
+        weight_y[i] = 0.5 * (conduct[i] + shift(conduct[i], -1, 1))
+        diagonal = weight_x[i] + weight_x[i + 1]
+        diagonal = diagonal + (weight_z[i] + shift(weight_z[i], 1, 0))
+        diagonal = diagonal + (weight_y[i] + shift(weight_y[i], 1, 1))
+        inside = conduct[i] > 0.0
+        inverse[i] = jnp.where(inside, 1.0 / jnp.where(inside, diagonal, 1.0), 0.0)
+
+    def operate_planes(field, low, high):
+        flux_x = [None] * (count + 1)
+        for i in range(low, high + 1):
+            if i == 0:
+                flux_x[i] = weight_x[i] * field[i]
+            elif i == count:
+                flux_x[i] = -(weight_x[i] * field[i - 1])
+            else:
+                flux_x[i] = weight_x[i] * (field[i] - field[i - 1])
+        result = [None] * count
+        for i in range(low, high):
+            flux_z = weight_z[i] * (field[i] - shift(field[i], -1, 0))
+            flux_y = weight_y[i] * (field[i] - shift(field[i], -1, 1))
+            result[i] = (
+                (flux_x[i] - flux_x[i + 1])
+                + (flux_z - shift(flux_z, 1, 0))
+                + (flux_y - shift(flux_y, 1, 1))
+            )
+        return result
+
+    low, high = edge, count - edge
+    residual = list(source)
+    if start is not None:
+        applied = operate_planes(start, low, high)
+        for i in range(low, high):
+            residual[i] = source[i] - applied[i]
+    direction = [None] * count
+    for i in range(low, high):
+        direction[i] = residual[i] * (inverse[i] * (1.0 / theta))
+    ratio_now = 1.0 / sigma
+    solution = list(start) if start is not None else [None] * count
+    for sweep_index in range(SWEEPS):
+        for i in range(low, high):
+            solution[i] = direction[i] if solution[i] is None else solution[i] + direction[i]
+        low, high = low + edge, high - edge
+        applied = operate_planes(direction, low, high)
+        for i in range(low, high):
+            residual[i] = residual[i] - applied[i]
+        if sweep_index + 1 < SWEEPS:
+            ratio_next = 1.0 / (2.0 * sigma - ratio_now)
+            turned = [None] * count
+            for i in range(low, high):
+                turned[i] = (ratio_next * ratio_now) * direction[i] + (
+                    2.0 * ratio_next / delta
+                ) * (residual[i] * inverse[i])
+            direction = turned
+            ratio_now = ratio_next
+    return solution, residual
+
+
+def split_dot(value, matrix):
+    parts = []
+    rest = value
+    for _ in range(3):
+        part = rest.astype(jnp.bfloat16)
+        parts.append(part.astype(jnp.float32))
+        rest = rest - parts[-1]
+    rows = value.shape[0]
+    stacked = jnp.concatenate(parts, axis=0).astype(jnp.bfloat16)
+    product = jnp.dot(stacked, matrix, preferred_element_type=jnp.float32)
+    return product[:rows] + product[rows : 2 * rows] + product[2 * rows :]
+
+
+def pair_matrix(keep_low, keep_high, offset):
+    source = lax.broadcasted_iota(jnp.int32, (LANES, LANES), 0)
+    target = lax.broadcasted_iota(jnp.int32, (LANES, LANES), 1)
+    low = (source < keep_low) & (target == offset + source // 2)
+    high = (source >= LANES - keep_high) & (target == LANES // 2 + source // 2)
+    return jnp.where(low | high, 1.0, 0.0).astype(jnp.bfloat16)
+
+
+def pair_rows(value, hold):
+    rows = value.shape[0]
+    hold[0:rows, :] = value
+    return hold[pl.ds(0, rows // 2, stride=2), :] + hold[pl.ds(1, rows // 2, stride=2), :]
+
+
+def kernel(sizes, *refs):
+    count_x, count_y, count_z = sizes
+    inputs = refs[0:3]
+    out_fine, out_one, out_two, out_three, out_rest = refs[3:8]
+    grown = refs[8:11]
+    (pack_full, pack_edge, pack_rows, got_full, got_edge, got_rows, own_one, own_half, all_one,
+     all_half, hold, solved_one, solved_fine, load_sem, face_send, face_recv, row_send, row_recv,
+     full_send, full_recv, edge_send, edge_recv, one_send, one_recv, store_sem) = refs[11:]
+    planes, rows = inputs[0].shape[0], inputs[0].shape[1]
+    x = lax.axis_index("gx")
+    y = lax.axis_index("gy")
+    z = lax.axis_index("gz")
+    first_z = z == 0
+
+    loads = []
+    for f in range(FIELDS):
+        loads.append(pltpu.make_async_copy(
+            inputs[f], grown[f].at[planes : 2 * planes, 0:rows, 0:LANES], load_sem.at[f]))
+        loads[-1].start()
+
+    def other(step, turn, dy):
+        return {"gx": lax.rem(x + step, count_x), "gy": y + dy, "gz": lax.rem(z + turn, count_z)}
+
+    partners = [
+        (step, turn, dy)
+        for step in range(count_x)
+        for turn in range(count_z)
+        for dy in (0, -1, 1)
+        if (step, turn, dy) != (0, 0, 0)
+    ]
+    barrier = pltpu.get_barrier_semaphore()
+    for dy in (0, -1, 1):
+        @pl.when(in_range(y + dy, count_y))
+        def _():
+            chosen = [p for p in partners if p[2] == dy]
+            for step, turn, _dy in chosen:
+                pl.semaphore_signal(
+                    barrier, inc=1, device_id=other(step, turn, dy),
+                    device_id_type=pl.DeviceIdType.MESH)
+
+    for f in range(FIELDS):
+        @pl.when(x == 0)
+        def _():
+            grown[f][0:planes, 0:rows, 0:LANES] = jnp.zeros((planes, rows, LANES), jnp.float32)
+
+        @pl.when(x == count_x - 1)
+        def _():
+            grown[f][2 * planes : 3 * planes, 0:rows, 0:LANES] = jnp.zeros(
+                (planes, rows, LANES), jnp.float32)
+
+    for slot in range(3):
+        for side in range(2):
+            there = in_range(x + (slot - 1), count_x) & in_range(y + (2 * side - 1), count_y)
+
+            @pl.when(jnp.logical_not(there))
+            def _():
+                got_full[slot, side] = jnp.zeros((rows, LANES), jnp.float32)
+                got_edge[slot, side] = jnp.zeros((ROWS, LANES), jnp.float32)
+
+        if slot != 1:
+            @pl.when(jnp.logical_not(in_range(x + (slot - 1), count_x)))
+            def _():
+                got_rows[slot] = jnp.zeros((FIELDS * planes, ROWS, LANES), jnp.float32)
+
+    for side in range(2):
+        @pl.when(jnp.logical_not(in_range(y + (2 * side - 1), count_y)))
+        def _():
+            for part in range(2):
+                all_half[part, side] = jnp.zeros(all_half.shape[2:], jnp.float32)
+
+    for load in loads:
+        load.wait()
+
+    lane = lax.broadcasted_iota(jnp.int32, (rows, LANES), 1)
+    packed = jnp.zeros((rows, LANES), jnp.float32)
+    for f in range(FIELDS):
+        for q in range(planes):
+            k = f * planes + q
+            piece = grown[f][planes + q, 0:rows, 0:LANES]
+            pack_rows[k] = jnp.where(first_z, piece[rows - ROWS :], piece[0:ROWS])
+            moved = shift(piece, 2 * WIDTH * k, 1)
+            window = lax.rem(lane - 2 * WIDTH * k + WIDTH + LANES, LANES) < 2 * WIDTH
+            packed = jnp.where(window, moved, packed)
+    pack_full[...] = packed
+    pack_edge[...] = jnp.where(first_z, packed[rows - ROWS :], packed[0:ROWS])
+
+    wanted = (count_x * count_z - 1) + count_x * count_z * (
+        jnp.where(y > 0, 1, 0) + jnp.where(y < count_y - 1, 1, 0))
+    pl.semaphore_wait(barrier, wanted)
+
+    started = []
+
+    def send(src, dst, send_sem, recv_sem, device, to, back):
+        copy = pltpu.make_async_remote_copy(
+            src_ref=src, dst_ref=dst, send_sem=send_sem, recv_sem=recv_sem,
+            device_id=device, device_id_type=pl.DeviceIdType.MESH)
+        if to is None:
+            copy.start()
+        else:
+            pl.when(to)(copy.start)
+        return copy, to, back
+
+    def wait_recv(entry):
+        copy, _, back = entry
+        if back is None:
+            copy.wait_recv()
+        else:
+            pl.when(back)(copy.wait_recv)
+
+    def wait_send(entry):
+        copy, to, _ = entry
+        if to is None:
+            copy.wait_send()
+        else:
+            pl.when(to)(copy.wait_send)
+
+    fine = []
+    for dx in (1, -1):
+        to, back = in_range(x + dx, count_x), in_range(x - dx, count_x)
+        for f in range(FIELDS):
+            low, high = 0, planes
+            if f == 2:
+                low, high = (1, planes) if dx == 1 else (0, planes - 1)
+            base = 0 if dx == 1 else 2 * planes
+            fine.append(send(
+                grown[f].at[planes + low : planes + high, 0:rows, 0:LANES],
+                grown[f].at[base + low : base + high, 0:rows, 0:LANES],
+                face_send.at[(dx + 1) // 2 * FIELDS + f], face_recv.at[(dx + 1) // 2 * FIELDS + f],
+                {"gx": x + dx, "gy": y, "gz": z}, to, back))
+    for dx in (0, 1, -1):
+        slot = 1 - dx
+        to, back = (in_range(x + dx, count_x), in_range(x - dx, count_x)) if dx else (None, None)
+        fine.append(send(
+            pack_rows, got_rows.at[slot], row_send.at[slot], row_recv.at[slot],
+            {"gx": x + dx, "gy": y, "gz": 1 - z}, to, back))
+    for dy in (1, -1):
+        side = (1 - dy) // 2
+        for dx in (0, 1, -1):
+            slot = 1 - dx
+            to = in_range(x + dx, count_x) & in_range(y + dy, count_y)
+            back = in_range(x - dx, count_x) & in_range(y - dy, count_y)
+            fine.append(send(
+                pack_full, got_full.at[slot, side], full_send.at[slot * 2 + side],
+                full_recv.at[slot * 2 + side], {"gx": x + dx, "gy": y + dy, "gz": z}, to, back))
+            fine.append(send(
+                pack_edge, got_edge.at[slot, side], edge_send.at[slot * 2 + side],
+                edge_recv.at[slot * 2 + side], {"gx": x + dx, "gy": y + dy, "gz": 1 - z}, to, back))
+
+    to_one = [pair_matrix(LANES, 0, 0), pair_matrix(LANES, 0, LANES // 2)]
+    matrix_one = jnp.concatenate(to_one, axis=0)
+    quarter = lax.broadcasted_iota(jnp.int32, (ROWS, LANES), 1) % (LANES // 2) < LANES // 4
+
+    def restrict_fine(blocks, scale):
+        pairs = [pair_rows(blocks[2 * q] + blocks[2 * q + 1], hold) for q in range(planes // 2)]
+        return scale * split_dot(jnp.concatenate(pairs, axis=1), matrix_one)
+
+    def spread(part, value):
+        own_one[part] = value
+        top, bottom = value[0:ROWS], value[ROWS : 2 * ROWS]
+        own_half[part, 0] = jnp.where(quarter, top, shift(bottom, LANES // 4, 1))
+        own_half[part, 1] = jnp.where(quarter, shift(bottom, -(LANES // 4), 1), top)
+        all_one[part, x, z] = value
+        entries = []
+        for index, (step, turn, dy) in enumerate(partners):
+            from_x, from_z = lax.rem(x + count_x - step, count_x), lax.rem(z + turn, count_z)
+            here = (part, x, z)
+            sems = (one_send.at[part, index], one_recv.at[part, index])
+            device = other(step, turn, dy)
+            if dy == 0:
+                entry = send(own_one.at[part], all_one.at[part, x, z], *sems, device, None, None)
+                landed = all_one.at[part, from_x, from_z]
+                source = own_one.at[part]
+                back = None
+            else:
+                side = (1 - dy) // 2
+                source = own_half.at[part, 0 if dy < 0 else 1]
+                entry = send(
+                    source, all_half.at[part, side, x, z], *sems, device,
+                    in_range(y + dy, count_y), None)
+                landed = all_half.at[part, side, from_x, from_z]
+                back = in_range(y - dy, count_y)
+            arrival = pltpu.make_async_remote_copy(
+                src_ref=source, dst_ref=landed, send_sem=sems[0], recv_sem=sems[1],
+                device_id=device, device_id_type=pl.DeviceIdType.MESH)
+            entries.append((entry, (arrival, None, back)))
+        return entries
+
+    conduct_entries = spread(
+        0, restrict_fine([grown[0][planes + q, 0:rows, 0:LANES] for q in range(planes)], 0.125))
+
+    for entry in fine:
+        wait_recv(entry)
+
+    row_index = lax.broadcasted_iota(jnp.int32, (ROWS, LANES), 0)
+    row_keep = (row_index < WIDTH) == first_z
+    lane_edge = lax.broadcasted_iota(jnp.int32, (rows + ROWS, LANES), 1)
+    lane_keep = (lane_edge < WIDTH) | (lane_edge >= LANES - WIDTH)
+    from_high = lax.rem(lane_edge, 2 * WIDTH) < WIDTH
+    for slot in range(3):
+        halves = []
+        for side in range(2):
+            halves.append(jnp.concatenate(
+                [got_full[slot, side], jnp.where(row_keep, got_edge[slot, side], 0.0)], axis=0))
+        joined = jnp.where(from_high, halves[1], halves[0])
+        for f in range(FIELDS):
+            for q in range(planes):
+                k = f * planes + q
+                p = slot * planes + q
+                grown[f][p, rows : rows + ROWS, 0:LANES] = jnp.where(row_keep, got_rows[slot, k], 0.0)
+                grown[f][p, :, LANES : 2 * LANES] = jnp.where(
+                    lane_keep, shift(joined, -2 * WIDTH * k, 1), 0.0)
+
+    solved, residual = smooth_planes(
+        [grown[0][p] for p in range(3 * planes)],
+        [None] + [grown[2][p] for p in range(1, 3 * planes - 1)] + [None],
+        [grown[1][p] for p in range(3 * planes)],
+        True,
+    )
+    source_entries = spread(
+        1, restrict_fine([residual[planes + q][0:rows, 0:LANES] for q in range(planes)], 0.25))
+    for q in range(planes):
+        solved_fine[q] = solved[planes + q][0:rows, 0:LANES]
+    store = pltpu.make_async_copy(solved_fine, out_fine, store_sem)
+    store.start()
+
+    lane_one = lax.broadcasted_iota(jnp.int32, (2 * ROWS, LANES), 1)
+    lower = lane_one < LANES // 2
+    empty = jnp.zeros((ROWS, LANES), jnp.float32)
+
+    def assemble(part):
+        level = []
+        for from_x in range(count_x):
+            blocks = [[], []]
+            for from_z in range(count_z):
+                own = all_one[part, from_x, from_z]
+                low, high = all_half[part, 0, from_x, from_z], all_half[part, 1, from_x, from_z]
+                beside = jnp.concatenate(
+                    [jnp.where(quarter, high, low),
+                     jnp.where(quarter, shift(high, -(LANES // 4), 1), shift(low, LANES // 4, 1))],
+                    axis=0)
+                blocks[0].append(jnp.where(lower, own, shift(beside, LANES // 2, 1)))
+                blocks[1].append(jnp.where(lower, shift(own, LANES // 2, 1), beside))
+            for q in range(2):
+                level.append(jnp.concatenate(blocks[q] + [empty], axis=0))
+        return level
+
+    def restrict(level, matrix, scale):
+        length = level[0].shape[0] - ROWS
+        summed = []
+        for q in range(len(level) // 2):
+            both = level[2 * q] + level[2 * q + 1]
+            summed.append(pair_rows(both[0:length], hold))
+        joined = scale * split_dot(jnp.concatenate(summed, axis=0), matrix)
+        half = length // 2
+        return [
+            jnp.concatenate([joined[q * half : (q + 1) * half], empty], axis=0)
+            for q in range(len(summed))
+        ]
+
+    matrix_two = pair_matrix(3 * LANES // 4, LANES // 4, 0)
+    matrix_three = pair_matrix(3 * LANES // 8, LANES // 8, 0)
+    for _, arrival in conduct_entries:
+        wait_recv(arrival)
+    conduct_one = assemble(0)
+    conduct_two = restrict(conduct_one, matrix_two, 0.125)
+    conduct_three = restrict(conduct_two, matrix_three, 0.125)
+
+    for _, arrival in source_entries:
+        wait_recv(arrival)
+    solved, residual = smooth_planes(conduct_one, assemble(1), None, False)
+    for p in range(len(solved)):
+        block = solved[p][0 : 2 * rows // 2]
+        solved_one[p] = jnp.where(first_z, block[0 : rows // 2], block[rows // 2 : rows])
+    out_one[...] = solved_one[pl.ds(2 * x, 2), :, 0 : LANES // 2]
+    solved, residual = smooth_planes(
+        conduct_two, restrict(residual, matrix_two, 0.25), None, False)
+    for p in range(len(solved)):
+        half = rows // 4
+        out_two[p] = jnp.where(first_z, solved[p][0:half], solved[p][half : 2 * half])[:, 0 : LANES // 4]
+    solved, residual = smooth_planes(
+        conduct_three, restrict(residual, matrix_three, 0.25), None, False)
+    for p in range(len(solved)):
+        half = rows // 8
+        for result, out in ((solved, out_three), (residual, out_rest)):
+            out[p] = jnp.where(first_z, result[p][0:half], result[p][half : 2 * half])[:, 0 : LANES // 8]
+
+    for entry in fine:
+        wait_send(entry)
+    for entry, _ in conduct_entries + source_entries:
+        wait_send(entry)
+    store.wait()
+
+
+def fits(mesh, shape):
+    return (
+        mesh.shape["gz"] == 2
+        and mesh.shape["gx"] <= 4
+        and shape[0] == WIDTH * mesh.shape["gx"]
+        and shape[1] == 32 * mesh.shape["gz"]
+        and shape[2] == LANES * mesh.shape["gy"]
+    )
+
+
+def fused(mesh, conductivity, initial_guess, right_side):
+    sizes = (mesh.shape["gx"], mesh.shape["gy"], mesh.shape["gz"])
+    count_x, _, count_z = sizes
+    planes, rows, lanes = conductivity.shape
+    f32 = jnp.float32
+    shapes = [
+        (planes, rows, lanes),
+        (planes // 2, rows // 2, lanes // 2),
+        (count_x * planes // 4, rows // 4, lanes // 4),
+        (count_x * planes // 8, rows // 8, lanes // 8),
+        (count_x * planes // 8, rows // 8, lanes // 8),
+    ]
+    others = 3 * count_x * count_z - 1
+    dma = pltpu.SemaphoreType.DMA
+    scratch = [pltpu.VMEM((3 * planes, rows + ROWS, 2 * LANES), f32)] * FIELDS + [
+        pltpu.VMEM((rows, LANES), f32),
+        pltpu.VMEM((ROWS, LANES), f32),
+        pltpu.VMEM((FIELDS * planes, ROWS, LANES), f32),
+        pltpu.VMEM((3, 2, rows, LANES), f32),
+        pltpu.VMEM((3, 2, ROWS, LANES), f32),
+        pltpu.VMEM((3, FIELDS * planes, ROWS, LANES), f32),
+        pltpu.VMEM((2, rows // 2, LANES), f32),
+        pltpu.VMEM((2, 2, ROWS, LANES), f32),
+        pltpu.VMEM((2, count_x, count_z, rows // 2, LANES), f32),
+        pltpu.VMEM((2, 2, count_x, count_z, ROWS, LANES), f32),
+        pltpu.VMEM((rows, LANES), f32),
+        pltpu.VMEM((2 * count_x, rows // 2, LANES), f32),
+        pltpu.VMEM((planes, rows, LANES), f32),
+        dma((3,)),
+        dma((6,)), dma((6,)),
+        dma((3,)), dma((3,)),
+        dma((6,)), dma((6,)),
+        dma((6,)), dma((6,)),
+        dma((2, others)), dma((2, others)),
+        dma,
+    ]
+    vmem = pl.BlockSpec(memory_space=pltpu.VMEM)
+    anywhere = pl.BlockSpec(memory_space=pl.ANY)
+    return pl.pallas_call(
+        functools.partial(kernel, sizes),
+        out_shape=[jax.ShapeDtypeStruct(shape, f32) for shape in shapes],
+        in_specs=[anywhere] * 3,
+        out_specs=[anywhere] + [vmem] * 4,
+        scratch_shapes=scratch,
+        compiler_params=pltpu.CompilerParams(
+            collective_id=0, has_side_effects=True, vmem_limit_bytes=32 * 2**20),
+    )(conductivity, initial_guess, right_side)
+
+
 def solution(mesh):
     placed = (P("gx", "gz", "gy"), P("gx", "gz", "gy"), P("gx", "gz", "gy"))
-    return jax.shard_map(
-        shards,
-        mesh=mesh,
-        in_specs=placed,
-        out_specs=(
-            P("gx", "gz", "gy"),
-            P("gx", "gz", "gy"),
-            P(None, "gz", "gy"),
-            P(None, "gz", "gy"),
-            P(None, "gz", "gy"),
-        ),
-        check_vma=False,
-    )
+
+    def whole(conductivity, initial_guess, right_side):
+        local = shards
+        if fits(mesh, conductivity.shape):
+            local = functools.partial(fused, mesh)
+        return jax.shard_map(
+            local,
+            mesh=mesh,
+            in_specs=placed,
+            out_specs=(
+                P("gx", "gz", "gy"),
+                P("gx", "gz", "gy"),
+                P(None, "gz", "gy"),
+                P(None, "gz", "gy"),
+                P(None, "gz", "gy"),
+            ),
+            check_vma=False,
+        )(conductivity, initial_guess, right_side)
+
+    return whole

time: 178 us -> 31 us (0.17)
  the two profiles are of different devices: /device:TPU:14 before, /device:TPU:0 now
where the time goes in v1:
time: 31 us; the launch traced here: 30.7 us
  Pallas kernels  24.5 us (79%)
  local copies, waits for them, and re-layouts  5.54 us (18%)
  between operations  0.65 us (2%)
    pallas_call x1, Pallas kernels, fused(): pl.pallas_call(functools.partial(kernel, sizes), out_shape=[jax.ShapeDtyp...  24.5 us
    unnamed x11, local copies, waits for them, and re-layouts  5.54 us

profile of v1, /device:TPU:0, one launch (start us, length us, event | category | flops | bytes accessed | tf_op | source)
XLA Modules:
  0.0 30.7 jit_solution(17094348851273935110)
XLA Ops:
  0.6 0.0 copy-start
  0.6 0.8 %copy-done = f32[4,32,128]{2,1,0:T(8,128)S(1)} copy-done((f32[4,32,128]{2,1,0:T(8,128)S(1)}, f32[4,32,128]{2,1,0:T(8,128)}, u32[]{:S(2)}) %copy-start) | copy-done | bytes 65560
  1.5 0.0 copy-start.1
  1.5 0.8 %copy-done.1 = f32[4,32,128]{2,1,0:T(8,128)S(1)} copy-done((f32[4,32,128]{2,1,0:T(8,128)S(1)}, f32[4,32,128]{2,1,0:T(8,128)}, u32[]{:S(2)}) %copy-start.1) | copy-done | bytes 65560
  2.3 0.0 copy-start.2
  2.3 0.8 %copy-done.2 = f32[4,32,128]{2,1,0:T(8,128)S(1)} copy-done((f32[4,32,128]{2,1,0:T(8,128)S(1)}, f32[4,32,128]{2,1,0:T(8,128)}, u32[]{:S(2)}) %copy-start.2) | copy-done | bytes 65560
  3.2 24.5 %shard_map.74 = (f32[4,32,128]{2,1,0:T(8,128)S(1)}, f32[2,16,64]{2,1,0:T(8,128)S(1)}, f32[4,8,32]{2,1,0:T(8,128)S(1)}, f32[2,4,16]{2,1,0:T(4,128)S(1)}, f32[2,4,16]{2,1,0:T(4,128)S(1)}) custom-call(f32[4,32,128]{2,1,0:T(8,128)S(1)} %copy-done, f32[4,32,128]{2,1,0:T(8,128)S(1)} %copy-done.1, f32[4,32,128]{2,1,0:T(8,128)S(1)} %copy-done.2), custom_call_target="tpu_custom_call" | custom-call | tf_op jit(solution)/shard_map/pallas_call | solution.py:625
  27.7 0.6 %copy.13 = f32[4,32,128]{2,1,0:T(8,128)} copy(f32[4,32,128]{2,1,0:T(8,128)S(1)} %get-tuple-element.10) | data formatting | bytes 131072
  28.3 0.6 %copy.14 = f32[2,16,64]{2,1,0:T(8,128)} copy(f32[2,16,64]{2,1,0:T(8,128)S(1)} %get-tuple-element.11) | data formatting | bytes 16384
  28.9 0.6 %copy.15 = f32[4,8,32]{2,1,0:T(8,128)} copy(f32[4,8,32]{2,1,0:T(8,128)S(1)} %get-tuple-element.12) | data formatting | bytes 8192
  29.5 0.6 %copy.16 = f32[2,4,16]{2,1,0:T(4,128)} copy(f32[2,4,16]{2,1,0:T(4,128)S(1)} %get-tuple-element.13) | data formatting | bytes 1024
  30.1 0.6 %copy.17 = f32[2,4,16]{2,1,0:T(4,128)} copy(f32[2,4,16]{2,1,0:T(4,128)S(1)} %get-tuple-element.14) | data formatting | bytes 1024
Async XLA Ops:
  0.6 0.8 %copy-start = (f32[4,32,128]{2,1,0:T(8,128)S(1)}, f32[4,32,128]{2,1,0:T(8,128)}, u32[]{:S(2)}) copy-start(f32[4,32,128]{2,1,0:T(8,128)} %refs_0_.1) | copy-start | bytes 196612
  1.5 0.8 %copy-start.1 = (f32[4,32,128]{2,1,0:T(8,128)S(1)}, f32[4,32,128]{2,1,0:T(8,128)}, u32[]{:S(2)}) copy-start(f32[4,32,128]{2,1,0:T(8,128)} %refs_1_.1) | copy-start | bytes 196612
  2.3 0.8 %copy-start.2 = (f32[4,32,128]{2,1,0:T(8,128)S(1)}, f32[4,32,128]{2,1,0:T(8,128)}, u32[]{:S(2)}) copy-start(f32[4,32,128]{2,1,0:T(8,128)} %refs_2_.1) | copy-start | bytes 196612

commit v2 on v1

--- a/solution.py
+++ b/solution.py
@@ -180,10 +180,7 @@
     return pltpu.roll(value, amount % value.shape[axis], axis)
 
 
-def smooth_planes(conduct, source, start, grown):
-    theta = 0.5 * (upper_bound + lower_bound)
-    delta = 0.5 * (upper_bound - lower_bound)
-    sigma = theta / delta
+def face_planes(conduct, grown):
     count = len(conduct)
     edge = 1 if grown else 0
     weight_x = [None] * (count + 1)
@@ -203,31 +200,43 @@
         diagonal = diagonal + (weight_y[i] + shift(weight_y[i], 1, 1))
         inside = conduct[i] > 0.0
         inverse[i] = jnp.where(inside, 1.0 / jnp.where(inside, diagonal, 1.0), 0.0)
-
-    def operate_planes(field, low, high):
-        flux_x = [None] * (count + 1)
-        for i in range(low, high + 1):
-            if i == 0:
-                flux_x[i] = weight_x[i] * field[i]
-            elif i == count:
-                flux_x[i] = -(weight_x[i] * field[i - 1])
-            else:
-                flux_x[i] = weight_x[i] * (field[i] - field[i - 1])
-        result = [None] * count
-        for i in range(low, high):
-            flux_z = weight_z[i] * (field[i] - shift(field[i], -1, 0))
-            flux_y = weight_y[i] * (field[i] - shift(field[i], -1, 1))
-            result[i] = (
-                (flux_x[i] - flux_x[i + 1])
-                + (flux_z - shift(flux_z, 1, 0))
-                + (flux_y - shift(flux_y, 1, 1))
-            )
-        return result
-
+    return weight_x, weight_y, weight_z, inverse
+
+
+def operate_planes(faces, field, low, high):
+    weight_x, weight_y, weight_z, _ = faces
+    count = len(field)
+    flux_x = [None] * (count + 1)
+    for i in range(low, high + 1):
+        if i == 0:
+            flux_x[i] = weight_x[i] * field[i]
+        elif i == count:
+            flux_x[i] = -(weight_x[i] * field[i - 1])
+        else:
+            flux_x[i] = weight_x[i] * (field[i] - field[i - 1])
+    result = [None] * count
+    for i in range(low, high):
+        flux_z = weight_z[i] * (field[i] - shift(field[i], -1, 0))
+        flux_y = weight_y[i] * (field[i] - shift(field[i], -1, 1))
+        result[i] = (
+            (flux_x[i] - flux_x[i + 1])
+            + (flux_z - shift(flux_z, 1, 0))
+            + (flux_y - shift(flux_y, 1, 1))
+        )
+    return result
+
+
+def smooth_planes(faces, source, start, grown):
+    theta = 0.5 * (upper_bound + lower_bound)
+    delta = 0.5 * (upper_bound - lower_bound)
+    sigma = theta / delta
+    inverse = faces[3]
+    count = len(source)
+    edge = 1 if grown else 0
     low, high = edge, count - edge
     residual = list(source)
     if start is not None:
-        applied = operate_planes(start, low, high)
+        applied = operate_planes(faces, start, low, high)
         for i in range(low, high):
             residual[i] = source[i] - applied[i]
     direction = [None] * count
@@ -239,7 +248,7 @@
         for i in range(low, high):
             solution[i] = direction[i] if solution[i] is None else solution[i] + direction[i]
         low, high = low + edge, high - edge
-        applied = operate_planes(direction, low, high)
+        applied = operate_planes(faces, direction, low, high)
         for i in range(low, high):
             residual[i] = residual[i] - applied[i]
         if sweep_index + 1 < SWEEPS:
@@ -284,11 +293,14 @@
 def kernel(sizes, *refs):
     count_x, count_y, count_z = sizes
     inputs = refs[0:3]
-    out_fine, out_one, out_two, out_three, out_rest = refs[3:8]
+    outs = refs[3:8]
     grown = refs[8:11]
     (pack_full, pack_edge, pack_rows, got_full, got_edge, got_rows, own_one, own_half, all_one,
-     all_half, hold, solved_one, solved_fine, load_sem, face_send, face_recv, row_send, row_recv,
+     all_half, hold, solved_one, out_fine, out_one, out_two,
+     out_three, out_rest, load_sem, face_send, face_recv, row_send, row_recv,
      full_send, full_recv, edge_send, edge_recv, one_send, one_recv, store_sem) = refs[11:]
+    kept = (out_fine, out_one, out_two, out_three, out_rest)
+    stores = [pltpu.make_async_copy(kept[i], outs[i], store_sem.at[i]) for i in range(5)]
     planes, rows = inputs[0].shape[0], inputs[0].shape[1]
     x = lax.axis_index("gx")
     y = lax.axis_index("gy")
@@ -493,8 +505,9 @@
                 grown[f][p, :, LANES : 2 * LANES] = jnp.where(
                     lane_keep, shift(joined, -2 * WIDTH * k, 1), 0.0)
 
+    faces = face_planes([grown[0][p] for p in range(3 * planes)], True)
     solved, residual = smooth_planes(
-        [grown[0][p] for p in range(3 * planes)],
+        faces,
         [None] + [grown[2][p] for p in range(1, 3 * planes - 1)] + [None],
         [grown[1][p] for p in range(3 * planes)],
         True,
@@ -502,9 +515,8 @@
     source_entries = spread(
         1, restrict_fine([residual[planes + q][0:rows, 0:LANES] for q in range(planes)], 0.25))
     for q in range(planes):
-        solved_fine[q] = solved[planes + q][0:rows, 0:LANES]
-    store = pltpu.make_async_copy(solved_fine, out_fine, store_sem)
-    store.start()
+        out_fine[q] = solved[planes + q][0:rows, 0:LANES]
+    stores[0].start()
 
     lane_one = lax.broadcasted_iota(jnp.int32, (2 * ROWS, LANES), 1)
     lower = lane_one < LANES // 2
@@ -547,31 +559,48 @@
     conduct_one = assemble(0)
     conduct_two = restrict(conduct_one, matrix_two, 0.125)
     conduct_three = restrict(conduct_two, matrix_three, 0.125)
+    faces_one, faces_two, faces_three = (
+        face_planes(conduct, False) for conduct in (conduct_one, conduct_two, conduct_three))
 
     for _, arrival in source_entries:
         wait_recv(arrival)
-    solved, residual = smooth_planes(conduct_one, assemble(1), None, False)
+    solved, residual = smooth_planes(faces_one, assemble(1), None, False)
     for p in range(len(solved)):
         block = solved[p][0 : 2 * rows // 2]
         solved_one[p] = jnp.where(first_z, block[0 : rows // 2], block[rows // 2 : rows])
     out_one[...] = solved_one[pl.ds(2 * x, 2), :, 0 : LANES // 2]
+    stores[1].start()
     solved, residual = smooth_planes(
-        conduct_two, restrict(residual, matrix_two, 0.25), None, False)
+        faces_two, restrict(residual, matrix_two, 0.25), None, False)
     for p in range(len(solved)):
         half = rows // 4
         out_two[p] = jnp.where(first_z, solved[p][0:half], solved[p][half : 2 * half])[:, 0 : LANES // 4]
+    stores[2].start()
     solved, residual = smooth_planes(
-        conduct_three, restrict(residual, matrix_three, 0.25), None, False)
+        faces_three, restrict(residual, matrix_three, 0.25), None, False)
     for p in range(len(solved)):
         half = rows // 8
         for result, out in ((solved, out_three), (residual, out_rest)):
             out[p] = jnp.where(first_z, result[p][0:half], result[p][half : 2 * half])[:, 0 : LANES // 8]
 
+    stores[3].start()
+    stores[4].start()
     for entry in fine:
         wait_send(entry)
     for entry, _ in conduct_entries + source_entries:
         wait_send(entry)
-    store.wait()
+    for store in stores:
+        store.wait()
+
+
+def hand_over(*refs):
+    count = len(refs) // 2
+    copies = []
+    for i in range(count):
+        copies.append(pltpu.make_async_copy(refs[i], refs[count + i], refs[-1].at[i]))
+        copies[-1].start()
+    for copy in copies:
+        copy.wait()
 
 
 def fits(mesh, shape):
@@ -611,26 +640,34 @@
         pltpu.VMEM((2, 2, count_x, count_z, ROWS, LANES), f32),
         pltpu.VMEM((rows, LANES), f32),
         pltpu.VMEM((2 * count_x, rows // 2, LANES), f32),
-        pltpu.VMEM((planes, rows, LANES), f32),
+        *[pltpu.VMEM(shape, f32) for shape in shapes],
         dma((3,)),
         dma((6,)), dma((6,)),
         dma((3,)), dma((3,)),
         dma((6,)), dma((6,)),
         dma((6,)), dma((6,)),
         dma((2, others)), dma((2, others)),
-        dma,
+        dma((5,)),
     ]
-    vmem = pl.BlockSpec(memory_space=pltpu.VMEM)
-    anywhere = pl.BlockSpec(memory_space=pl.ANY)
-    return pl.pallas_call(
+    outside = pl.BlockSpec(memory_space=pltpu.HBM)
+    out_shape = [jax.ShapeDtypeStruct(shape, f32) for shape in shapes]
+    results = pl.pallas_call(
         functools.partial(kernel, sizes),
-        out_shape=[jax.ShapeDtypeStruct(shape, f32) for shape in shapes],
-        in_specs=[anywhere] * 3,
-        out_specs=[anywhere] + [vmem] * 4,
+        out_shape=out_shape,
+        in_specs=[outside] * 3,
+        out_specs=[outside] * 5,
         scratch_shapes=scratch,
         compiler_params=pltpu.CompilerParams(
-            collective_id=0, has_side_effects=True, vmem_limit_bytes=32 * 2**20),
+            collective_id=0, has_side_effects=True, vmem_limit_bytes=56 * 2**20),
     )(conductivity, initial_guess, right_side)
+    return pl.pallas_call(
+        hand_over,
+        out_shape=out_shape,
+        in_specs=[outside] * 5,
+        out_specs=[outside] * 5,
+        scratch_shapes=[dma((5,))],
+        compiler_params=pltpu.CompilerParams(vmem_limit_bytes=56 * 2**20),
+    )(*results)
 
 
 def solution(mesh):

time: 31 us -> 30.2 us (0.974)
  local copies, waits for them, and re-layouts: 5.54 us -> 0 us
  Pallas kernels: 24.5 us -> 29.4 us
    unnamed x11 -> x0, local copies, waits for them, and re-layouts: 5.54 us -> none
    pallas_call x1 -> x2, Pallas kernels: 24.5 us -> 29.4 us  [the longest x1 25 us: fused(): pl.pallas_call(functools.partial(kernel, sizes), out_shape=out_shape, in_...]
where the time goes in v2:
time: 30.2 us; the launch traced here: 30.1 us
  Pallas kernels  29.4 us (97%)
  between operations  0.64 us (2%)
    pallas_call x1, Pallas kernels, fused(): pl.pallas_call(functools.partial(kernel, sizes), out_shape=out_shape, in_...  25 us
    pallas_call x1, Pallas kernels, fused(): pl.pallas_call(hand_over, out_shape=out_shape, in_specs=[outside] * 5, ou...  4.38 us

profile of v2, /device:TPU:0, one launch (start us, length us, event | category | flops | bytes accessed | tf_op | source)
XLA Modules:
  0.0 30.1 jit_solution(15510975181709854296)
XLA Ops:
  0.6 25.0 %shard_map.74 = (f32[4,32,128]{2,1,0:T(8,128)}, f32[2,16,64]{2,1,0:T(8,128)}, f32[4,8,32]{2,1,0:T(8,128)}, f32[2,4,16]{2,1,0:T(4,128)}, f32[2,4,16]{2,1,0:T(4,128)}) custom-call(f32[4,32,128]{2,1,0:T(8,128)} %refs_0_.1, f32[4,32,128]{2,1,0:T(8,128)} %refs_1_.1, f32[4,32,128]{2,1,0:T(8,128)} %refs_2_.1), custom_call_target="tpu_custom_call" | custom-call | tf_op jit(solution)/shard_map/pallas_call | solution.py:654
  25.7 4.4 %shard_map.75 = (f32[4,32,128]{2,1,0:T(8,128)}, f32[2,16,64]{2,1,0:T(8,128)}, f32[4,8,32]{2,1,0:T(8,128)}, f32[2,4,16]{2,1,0:T(4,128)}, f32[2,4,16]{2,1,0:T(4,128)}) custom-call(f32[4,32,128]{2,1,0:T(8,128)} %get-tuple-element.10.refs_0_, f32[2,16,64]{2,1,0:T(8,128)} %get-tuple-element.11.refs_1_, f32[4,8,32]{2,1,0:T(8,128)} %get-tuple-element.12.refs_2_, ...), custom_call_target="tpu_custom_call" | custom-call | tf_op jit(solution)/shard_map/pallas_call | solution.py:663

commit v3 on v2

--- a/solution.py
+++ b/solution.py
@@ -226,19 +226,15 @@
     return result
 
 
-def smooth_planes(faces, source, start, grown):
+def smooth_planes(faces, residual, start, grown):
     theta = 0.5 * (upper_bound + lower_bound)
     delta = 0.5 * (upper_bound - lower_bound)
     sigma = theta / delta
     inverse = faces[3]
-    count = len(source)
+    count = len(residual)
     edge = 1 if grown else 0
     low, high = edge, count - edge
-    residual = list(source)
-    if start is not None:
-        applied = operate_planes(faces, start, low, high)
-        for i in range(low, high):
-            residual[i] = source[i] - applied[i]
+    residual = list(residual)
     direction = [None] * count
     for i in range(low, high):
         direction[i] = residual[i] * (inverse[i] * (1.0 / theta))
@@ -316,6 +312,14 @@
     def other(step, turn, dy):
         return {"gx": lax.rem(x + step, count_x), "gy": y + dy, "gz": lax.rem(z + turn, count_z)}
 
+    near = planes - WIDTH
+    strip_list = [
+        [(f, q) for f in range(FIELDS) for q in range(planes)
+         if q > near + (1 if f == 2 else 0)],
+        [(f, q) for f in range(FIELDS) for q in range(planes)],
+        [(f, q) for f in range(FIELDS) for q in range(planes)
+         if q < WIDTH - 1 - (1 if f == 2 else 0)],
+    ]
     partners = [
         (step, turn, dy)
         for step in range(count_x)
@@ -349,13 +353,13 @@
 
             @pl.when(jnp.logical_not(there))
             def _():
-                got_full[slot, side] = jnp.zeros((rows, LANES), jnp.float32)
+                got_full[slot, side] = jnp.zeros((rows // 2, LANES), jnp.float32)
                 got_edge[slot, side] = jnp.zeros((ROWS, LANES), jnp.float32)
 
         if slot != 1:
             @pl.when(jnp.logical_not(in_range(x + (slot - 1), count_x)))
             def _():
-                got_rows[slot] = jnp.zeros((FIELDS * planes, ROWS, LANES), jnp.float32)
+                got_rows[slot] = jnp.zeros(got_rows.shape[1:], jnp.float32)
 
     for side in range(2):
         @pl.when(jnp.logical_not(in_range(y + (2 * side - 1), count_y)))
@@ -367,23 +371,32 @@
         load.wait()
 
     lane = lax.broadcasted_iota(jnp.int32, (rows, LANES), 1)
+    row_index = lax.broadcasted_iota(jnp.int32, (ROWS, LANES), 0)
+    low_lane = lax.rem(lane[0 : rows // 2], 2 * WIDTH) < WIDTH
+    leave = (row_index < WIDTH) == jnp.logical_not(first_z)
+    strips = {}
     packed = jnp.zeros((rows, LANES), jnp.float32)
     for f in range(FIELDS):
         for q in range(planes):
             k = f * planes + q
             piece = grown[f][planes + q, 0:rows, 0:LANES]
-            pack_rows[k] = jnp.where(first_z, piece[rows - ROWS :], piece[0:ROWS])
+            strips[f, q] = jnp.where(first_z, piece[rows - ROWS :], piece[0:ROWS])
             moved = shift(piece, 2 * WIDTH * k, 1)
             window = lax.rem(lane - 2 * WIDTH * k + WIDTH + LANES, LANES) < 2 * WIDTH
             packed = jnp.where(window, moved, packed)
-    pack_full[...] = packed
+    for slot in range(3):
+        for t in range(len(strip_list[slot]) // 2):
+            first, second = strip_list[slot][2 * t], strip_list[slot][2 * t + 1]
+            pack_rows[slot, t] = jnp.where(
+                leave, strips[first], shift(strips[second], WIDTH, 0))
+    top, bottom = packed[0 : rows // 2], packed[rows // 2 : rows]
+    pack_full[0] = jnp.where(low_lane, shift(bottom, -WIDTH, 1), top)
+    pack_full[1] = jnp.where(low_lane, top, shift(bottom, WIDTH, 1))
     pack_edge[...] = jnp.where(first_z, packed[rows - ROWS :], packed[0:ROWS])
 
     wanted = (count_x * count_z - 1) + count_x * count_z * (
         jnp.where(y > 0, 1, 0) + jnp.where(y < count_y - 1, 1, 0))
     pl.semaphore_wait(barrier, wanted)
-
-    started = []
 
     def send(src, dst, send_sem, recv_sem, device, to, back):
         copy = pltpu.make_async_remote_copy(
@@ -409,37 +422,43 @@
         else:
             pl.when(to)(copy.wait_send)
 
-    fine = []
-    for dx in (1, -1):
-        to, back = in_range(x + dx, count_x), in_range(x - dx, count_x)
-        for f in range(FIELDS):
+    faces = []
+    strips_sent = []
+
+    def send_face(f):
+        for dx in (1, -1):
+            to, back = in_range(x + dx, count_x), in_range(x - dx, count_x)
             low, high = 0, planes
             if f == 2:
                 low, high = (1, planes) if dx == 1 else (0, planes - 1)
             base = 0 if dx == 1 else 2 * planes
-            fine.append(send(
+            index = (dx + 1) // 2 * FIELDS + f
+            faces.append((f, send(
                 grown[f].at[planes + low : planes + high, 0:rows, 0:LANES],
                 grown[f].at[base + low : base + high, 0:rows, 0:LANES],
-                face_send.at[(dx + 1) // 2 * FIELDS + f], face_recv.at[(dx + 1) // 2 * FIELDS + f],
-                {"gx": x + dx, "gy": y, "gz": z}, to, back))
-    for dx in (0, 1, -1):
+                face_send.at[index], face_recv.at[index],
+                {"gx": x + dx, "gy": y, "gz": z}, to, back)))
+
+    send_face(0)
+    for dx in (1, -1, 0):
         slot = 1 - dx
         to, back = (in_range(x + dx, count_x), in_range(x - dx, count_x)) if dx else (None, None)
-        fine.append(send(
-            pack_rows, got_rows.at[slot], row_send.at[slot], row_recv.at[slot],
-            {"gx": x + dx, "gy": y, "gz": 1 - z}, to, back))
-    for dy in (1, -1):
-        side = (1 - dy) // 2
-        for dx in (0, 1, -1):
-            slot = 1 - dx
+        tiles = len(strip_list[slot]) // 2
+        strips_sent.append(send(
+            pack_rows.at[slot, 0:tiles], got_rows.at[slot, 0:tiles], row_send.at[slot],
+            row_recv.at[slot], {"gx": x + dx, "gy": y, "gz": 1 - z}, to, back))
+        for dy in (1, -1):
+            side = (1 - dy) // 2
             to = in_range(x + dx, count_x) & in_range(y + dy, count_y)
             back = in_range(x - dx, count_x) & in_range(y - dy, count_y)
-            fine.append(send(
-                pack_full, got_full.at[slot, side], full_send.at[slot * 2 + side],
+            strips_sent.append(send(
+                pack_full.at[side], got_full.at[slot, side], full_send.at[slot * 2 + side],
                 full_recv.at[slot * 2 + side], {"gx": x + dx, "gy": y + dy, "gz": z}, to, back))
-            fine.append(send(
+            strips_sent.append(send(
                 pack_edge, got_edge.at[slot, side], edge_send.at[slot * 2 + side],
                 edge_recv.at[slot * 2 + side], {"gx": x + dx, "gy": y + dy, "gz": 1 - z}, to, back))
+    send_face(1)
+    send_face(2)
 
     to_one = [pair_matrix(LANES, 0, 0), pair_matrix(LANES, 0, LANES // 2)]
     matrix_one = jnp.concatenate(to_one, axis=0)
@@ -449,70 +468,97 @@
         pairs = [pair_rows(blocks[2 * q] + blocks[2 * q + 1], hold) for q in range(planes // 2)]
         return scale * split_dot(jnp.concatenate(pairs, axis=1), matrix_one)
 
+    here = x * count_z + z
+    blocks_all = count_x * count_z
+
     def spread(part, value):
         own_one[part] = value
         top, bottom = value[0:ROWS], value[ROWS : 2 * ROWS]
-        own_half[part, 0] = jnp.where(quarter, top, shift(bottom, LANES // 4, 1))
-        own_half[part, 1] = jnp.where(quarter, shift(bottom, -(LANES // 4), 1), top)
-        all_one[part, x, z] = value
-        entries = []
-        for index, (step, turn, dy) in enumerate(partners):
-            from_x, from_z = lax.rem(x + count_x - step, count_x), lax.rem(z + turn, count_z)
-            here = (part, x, z)
-            sems = (one_send.at[part, index], one_recv.at[part, index])
-            device = other(step, turn, dy)
+        own_half[part, 0] = jnp.where(quarter, shift(bottom, -(LANES // 4), 1), top)
+        own_half[part, 1] = jnp.where(quarter, top, shift(bottom, LANES // 4, 1))
+        all_one[part, here] = value
+        for dy in (0, 1, -1):
+            side = (1 - dy) // 2
+
+            def start():
+                for step, turn, _dy in [p for p in partners if p[2] == dy]:
+                    if dy == 0:
+                        source, target = own_one.at[part], all_one.at[part, here]
+                    else:
+                        source, target = own_half.at[part, side], all_half.at[part, side, here]
+                    pltpu.make_async_remote_copy(
+                        src_ref=source, dst_ref=target, send_sem=one_send.at[part, dy + 1],
+                        recv_sem=one_recv.at[part, dy + 1], device_id=other(step, turn, dy),
+                        device_id_type=pl.DeviceIdType.MESH).start()
+
             if dy == 0:
-                entry = send(own_one.at[part], all_one.at[part, x, z], *sems, device, None, None)
-                landed = all_one.at[part, from_x, from_z]
-                source = own_one.at[part]
-                back = None
+                start()
             else:
-                side = (1 - dy) // 2
-                source = own_half.at[part, 0 if dy < 0 else 1]
-                entry = send(
-                    source, all_half.at[part, side, x, z], *sems, device,
-                    in_range(y + dy, count_y), None)
-                landed = all_half.at[part, side, from_x, from_z]
-                back = in_range(y - dy, count_y)
-            arrival = pltpu.make_async_remote_copy(
-                src_ref=source, dst_ref=landed, send_sem=sems[0], recv_sem=sems[1],
-                device_id=device, device_id_type=pl.DeviceIdType.MESH)
-            entries.append((entry, (arrival, None, back)))
-        return entries
-
-    conduct_entries = spread(
-        0, restrict_fine([grown[0][planes + q, 0:rows, 0:LANES] for q in range(planes)], 0.125))
-
-    for entry in fine:
+                pl.when(in_range(y + dy, count_y))(start)
+
+    def settle(part, received):
+        for dy in (0, 1, -1):
+            side = (1 - dy) // 2
+            bytes_of = all_one.at[part, 0 : blocks_all - 1] if dy == 0 else all_half.at[part, side]
+            copy = pltpu.make_async_remote_copy(
+                src_ref=bytes_of, dst_ref=bytes_of, send_sem=one_send.at[part, dy + 1],
+                recv_sem=one_recv.at[part, dy + 1], device_id=other(1, 0, 0),
+                device_id_type=pl.DeviceIdType.MESH)
+            finish = copy.wait_recv if received else copy.wait_send
+            if dy == 0:
+                finish()
+            else:
+                pl.when(in_range(y - dy if received else y + dy, count_y))(finish)
+
+    coarse_conduct = restrict_fine(
+        [grown[0][planes + q, 0:rows, 0:LANES] for q in range(planes)], 0.125)
+
+    for entry in strips_sent:
         wait_recv(entry)
-
-    row_index = lax.broadcasted_iota(jnp.int32, (ROWS, LANES), 0)
     row_keep = (row_index < WIDTH) == first_z
     lane_edge = lax.broadcasted_iota(jnp.int32, (rows + ROWS, LANES), 1)
     lane_keep = (lane_edge < WIDTH) | (lane_edge >= LANES - WIDTH)
-    from_high = lax.rem(lane_edge, 2 * WIDTH) < WIDTH
+    low_edge = low_lane[0:ROWS]
+    joined = []
     for slot in range(3):
-        halves = []
-        for side in range(2):
-            halves.append(jnp.concatenate(
-                [got_full[slot, side], jnp.where(row_keep, got_edge[slot, side], 0.0)], axis=0))
-        joined = jnp.where(from_high, halves[1], halves[0])
-        for f in range(FIELDS):
+        low, high = got_full[slot, 1], got_full[slot, 0]
+        joined.append(jnp.concatenate([
+            jnp.where(low_lane, low, high),
+            jnp.where(low_lane, shift(low, -WIDTH, 1), shift(high, WIDTH, 1)),
+            jnp.where(row_keep, jnp.where(low_edge, got_edge[slot, 1], got_edge[slot, 0]), 0.0),
+        ], axis=0))
+    for f in range(FIELDS):
+        for slot in range(3):
             for q in range(planes):
-                k = f * planes + q
                 p = slot * planes + q
-                grown[f][p, rows : rows + ROWS, 0:LANES] = jnp.where(row_keep, got_rows[slot, k], 0.0)
+                strip = jnp.zeros((ROWS, LANES), jnp.float32)
+                if (f, q) in strip_list[slot]:
+                    index = strip_list[slot].index((f, q))
+                    strip = got_rows[slot, index // 2]
+                    if index % 2 == 1:
+                        strip = shift(strip, WIDTH, 0)
+                    strip = jnp.where(row_keep, strip, 0.0)
+                grown[f][p, rows : rows + ROWS, 0:LANES] = strip
                 grown[f][p, :, LANES : 2 * LANES] = jnp.where(
-                    lane_keep, shift(joined, -2 * WIDTH * k, 1), 0.0)
-
-    faces = face_planes([grown[0][p] for p in range(3 * planes)], True)
-    solved, residual = smooth_planes(
-        faces,
-        [None] + [grown[2][p] for p in range(1, 3 * planes - 1)] + [None],
-        [grown[1][p] for p in range(3 * planes)],
-        True,
-    )
-    source_entries = spread(
+                    lane_keep, shift(joined[slot], -2 * WIDTH * (f * planes + q), 1), 0.0)
+
+    def wait_face(f):
+        for index, entry in faces:
+            if index == f:
+                wait_recv(entry)
+
+    wait_face(0)
+    faces_fine = face_planes([grown[0][p] for p in range(3 * planes)], True)
+    spread(0, coarse_conduct)
+    wait_face(1)
+    start = [grown[1][p] for p in range(3 * planes)]
+    applied = operate_planes(faces_fine, start, 1, 3 * planes - 1)
+    wait_face(2)
+    residual = [None] * (3 * planes)
+    for p in range(1, 3 * planes - 1):
+        residual[p] = grown[2][p] - applied[p]
+    solved, residual = smooth_planes(faces_fine, residual, start, True)
+    spread(
         1, restrict_fine([residual[planes + q][0:rows, 0:LANES] for q in range(planes)], 0.25))
     for q in range(planes):
         out_fine[q] = solved[planes + q][0:rows, 0:LANES]
@@ -527,8 +573,9 @@
         for from_x in range(count_x):
             blocks = [[], []]
             for from_z in range(count_z):
-                own = all_one[part, from_x, from_z]
-                low, high = all_half[part, 0, from_x, from_z], all_half[part, 1, from_x, from_z]
+                block = from_x * count_z + from_z
+                own = all_one[part, block]
+                low, high = all_half[part, 0, block], all_half[part, 1, block]
                 beside = jnp.concatenate(
                     [jnp.where(quarter, high, low),
                      jnp.where(quarter, shift(high, -(LANES // 4), 1), shift(low, LANES // 4, 1))],
@@ -554,16 +601,14 @@
 
     matrix_two = pair_matrix(3 * LANES // 4, LANES // 4, 0)
     matrix_three = pair_matrix(3 * LANES // 8, LANES // 8, 0)
-    for _, arrival in conduct_entries:
-        wait_recv(arrival)
+    settle(0, True)
     conduct_one = assemble(0)
     conduct_two = restrict(conduct_one, matrix_two, 0.125)
     conduct_three = restrict(conduct_two, matrix_three, 0.125)
     faces_one, faces_two, faces_three = (
         face_planes(conduct, False) for conduct in (conduct_one, conduct_two, conduct_three))
 
-    for _, arrival in source_entries:
-        wait_recv(arrival)
+    settle(1, True)
     solved, residual = smooth_planes(faces_one, assemble(1), None, False)
     for p in range(len(solved)):
         block = solved[p][0 : 2 * rows // 2]
@@ -585,10 +630,10 @@
 
     stores[3].start()
     stores[4].start()
-    for entry in fine:
+    for entry in strips_sent + [entry for _, entry in faces]:
         wait_send(entry)
-    for entry, _ in conduct_entries + source_entries:
-        wait_send(entry)
+    settle(0, False)
+    settle(1, False)
     for store in stores:
         store.wait()
 
@@ -625,19 +670,19 @@
         (count_x * planes // 8, rows // 8, lanes // 8),
         (count_x * planes // 8, rows // 8, lanes // 8),
     ]
-    others = 3 * count_x * count_z - 1
+    blocks_all = count_x * count_z
     dma = pltpu.SemaphoreType.DMA
     scratch = [pltpu.VMEM((3 * planes, rows + ROWS, 2 * LANES), f32)] * FIELDS + [
-        pltpu.VMEM((rows, LANES), f32),
+        pltpu.VMEM((2, rows // 2, LANES), f32),
         pltpu.VMEM((ROWS, LANES), f32),
-        pltpu.VMEM((FIELDS * planes, ROWS, LANES), f32),
-        pltpu.VMEM((3, 2, rows, LANES), f32),
+        pltpu.VMEM((3, FIELDS * planes // 2, ROWS, LANES), f32),
+        pltpu.VMEM((3, 2, rows // 2, LANES), f32),
         pltpu.VMEM((3, 2, ROWS, LANES), f32),
-        pltpu.VMEM((3, FIELDS * planes, ROWS, LANES), f32),
+        pltpu.VMEM((3, FIELDS * planes // 2, ROWS, LANES), f32),
         pltpu.VMEM((2, rows // 2, LANES), f32),
         pltpu.VMEM((2, 2, ROWS, LANES), f32),
-        pltpu.VMEM((2, count_x, count_z, rows // 2, LANES), f32),
-        pltpu.VMEM((2, 2, count_x, count_z, ROWS, LANES), f32),
+        pltpu.VMEM((2, blocks_all, rows // 2, LANES), f32),
+        pltpu.VMEM((2, 2, blocks_all, ROWS, LANES), f32),
         pltpu.VMEM((rows, LANES), f32),
         pltpu.VMEM((2 * count_x, rows // 2, LANES), f32),
         *[pltpu.VMEM(shape, f32) for shape in shapes],
@@ -646,7 +691,7 @@
         dma((3,)), dma((3,)),
         dma((6,)), dma((6,)),
         dma((6,)), dma((6,)),
-        dma((2, others)), dma((2, others)),
+        dma((2, 3)), dma((2, 3)),
         dma((5,)),
     ]
     outside = pl.BlockSpec(memory_space=pltpu.HBM)
@@ -663,7 +708,7 @@
     return pl.pallas_call(
         hand_over,
         out_shape=out_shape,
-        in_specs=[outside] * 5,
+        in_specs=[pl.BlockSpec(memory_space=pltpu.VMEM)] * 5,
         out_specs=[outside] * 5,
         scratch_shapes=[dma((5,))],
         compiler_params=pltpu.CompilerParams(vmem_limit_bytes=56 * 2**20),

time: 30.2 us -> 25.2 us (0.83)
  Pallas kernels: 29.4 us -> 24.3 us
    pallas_call x1, Pallas kernels: 4.38 us -> 1.55 us  [fused(): pl.pallas_call(hand_over, out_shape=out_shape, in_specs=[pl.BlockSpec(mem...]
    pallas_call x1, Pallas kernels: 25 us -> 22.8 us  [fused(): pl.pallas_call(functools.partial(kernel, sizes), out_shape=out_shape, in_...]
where the time goes in v3:
time: 25.2 us; the launch traced here: 24.9 us
  Pallas kernels  24.3 us (96%)
  between operations  0.64 us (3%)
    pallas_call x1, Pallas kernels, fused(): pl.pallas_call(functools.partial(kernel, sizes), out_shape=out_shape, in_...  22.8 us
    pallas_call x1, Pallas kernels, fused(): pl.pallas_call(hand_over, out_shape=out_shape, in_specs=[pl.BlockSpec(mem...  1.55 us

profile of v3, /device:TPU:0, one launch (start us, length us, event | category | flops | bytes accessed | tf_op | source)
XLA Modules:
  0.0 24.9 jit_solution(3856278123067599726)
XLA Ops:
  0.6 22.8 %shard_map.74 = (f32[4,32,128]{2,1,0:T(8,128)}, f32[2,16,64]{2,1,0:T(8,128)}, f32[4,8,32]{2,1,0:T(8,128)}, f32[2,4,16]{2,1,0:T(4,128)}, f32[2,4,16]{2,1,0:T(4,128)}) custom-call(f32[4,32,128]{2,1,0:T(8,128)} %refs_0_.1, f32[4,32,128]{2,1,0:T(8,128)} %refs_1_.1, f32[4,32,128]{2,1,0:T(8,128)} %refs_2_.1), custom_call_target="tpu_custom_call" | custom-call | tf_op jit(solution)/shard_map/pallas_call | solution.py:699
  23.4 1.5 %shard_map.75 = (f32[4,32,128]{2,1,0:T(8,128)}, f32[2,16,64]{2,1,0:T(8,128)}, f32[4,8,32]{2,1,0:T(8,128)}, f32[2,4,16]{2,1,0:T(4,128)}, f32[2,4,16]{2,1,0:T(4,128)}) custom-call(f32[4,32,128]{2,1,0:T(8,128)} %get-tuple-element.10.refs_0_, f32[2,16,64]{2,1,0:T(8,128)} %get-tuple-element.11.refs_1_, f32[4,8,32]{2,1,0:T(8,128)} %get-tuple-element.12.refs_2_, ...), custom_call_target="tpu_custom_call" | custom-call | tf_op jit(solution)/shard_map/pallas_call | solution.py:708

commit v4 on v3

--- a/solution.py
+++ b/solution.py
@@ -291,10 +291,10 @@
     inputs = refs[0:3]
     outs = refs[3:8]
     grown = refs[8:11]
-    (pack_full, pack_edge, pack_rows, got_full, got_edge, got_rows, own_one, own_half, all_one,
+    (pack_full, pack_edge, pack_rows, got_full, got_edge, got_rows, own_one, own_half, line_half, all_one,
      all_half, hold, solved_one, out_fine, out_one, out_two,
      out_three, out_rest, load_sem, face_send, face_recv, row_send, row_recv,
-     full_send, full_recv, edge_send, edge_recv, one_send, one_recv, store_sem) = refs[11:]
+     full_send, full_recv, edge_send, edge_recv, one_send, one_recv, hop_send, hop_recv, store_sem) = refs[11:]
     kept = (out_fine, out_one, out_two, out_three, out_rest)
     stores = [pltpu.make_async_copy(kept[i], outs[i], store_sem.at[i]) for i in range(5)]
     planes, rows = inputs[0].shape[0], inputs[0].shape[1]
@@ -468,7 +468,9 @@
         pairs = [pair_rows(blocks[2 * q] + blocks[2 * q + 1], hold) for q in range(planes // 2)]
         return scale * split_dot(jnp.concatenate(pairs, axis=1), matrix_one)
 
-    here = x * count_z + z
+    hopped = (0,)
+    here = z * count_x + x
+    line = pl.ds(z * count_x, count_x)
     blocks_all = count_x * count_z
 
     def spread(part, value):
@@ -496,14 +498,60 @@
             else:
                 pl.when(in_range(y + dy, count_y))(start)
 
+    def remote(source, target, send_sem, recv_sem, device):
+        return pltpu.make_async_remote_copy(
+            src_ref=source, dst_ref=target, send_sem=send_sem, recv_sem=recv_sem,
+            device_id=device, device_id_type=pl.DeviceIdType.MESH)
+
+    def first_hop(part, value):
+        own_one[part] = value
+        all_one[part, here] = value
+        for step in range(1, count_x):
+            remote(own_one.at[part], all_one.at[part, here], hop_send.at[part],
+                   hop_recv.at[part], other(step, 0, 0)).start()
+
+    def settle_hop(part, received):
+        bytes_of = all_one.at[part, 0 : count_x - 1]
+        copy = remote(bytes_of, bytes_of, hop_send.at[part], hop_recv.at[part], other(1, 0, 0))
+        copy.wait_recv() if received else copy.wait_send()
+
+    def line_copies(part, dy):
+        side = (1 - dy) // 2
+        sems = (one_send.at[part, dy + 1], one_recv.at[part, dy + 1])
+        if dy == 0:
+            return [remote(all_one.at[part, line], all_one.at[part, line], *sems, other(0, 1, 0))]
+        return [
+            remote(line_half.at[part, side], all_half.at[part, side, line], *sems,
+                   other(0, turn, dy))
+            for turn in range(count_z)
+        ]
+
+    def second_hop(part):
+        for from_x in range(count_x):
+            value = all_one[part, z * count_x + from_x]
+            top, bottom = value[0:ROWS], value[ROWS : 2 * ROWS]
+            line_half[part, 0, from_x] = jnp.where(quarter, shift(bottom, -(LANES // 4), 1), top)
+            line_half[part, 1, from_x] = jnp.where(quarter, top, shift(bottom, LANES // 4, 1))
+        for dy in (0, 1, -1):
+            def start():
+                for copy in line_copies(part, dy):
+                    copy.start()
+
+            if dy == 0:
+                start()
+            else:
+                pl.when(in_range(y + dy, count_y))(start)
+
     def settle(part, received):
         for dy in (0, 1, -1):
             side = (1 - dy) // 2
-            bytes_of = all_one.at[part, 0 : blocks_all - 1] if dy == 0 else all_half.at[part, side]
-            copy = pltpu.make_async_remote_copy(
-                src_ref=bytes_of, dst_ref=bytes_of, send_sem=one_send.at[part, dy + 1],
-                recv_sem=one_recv.at[part, dy + 1], device_id=other(1, 0, 0),
-                device_id_type=pl.DeviceIdType.MESH)
+            if dy == 0:
+                extent = count_x if part in hopped else blocks_all - 1
+                bytes_of = all_one.at[part, 0:extent]
+            else:
+                bytes_of = all_half.at[part, side]
+            copy = remote(bytes_of, bytes_of, one_send.at[part, dy + 1],
+                          one_recv.at[part, dy + 1], other(1, 0, 0))
             finish = copy.wait_recv if received else copy.wait_send
             if dy == 0:
                 finish()
@@ -512,6 +560,7 @@
 
     coarse_conduct = restrict_fine(
         [grown[0][planes + q, 0:rows, 0:LANES] for q in range(planes)], 0.125)
+    first_hop(0, coarse_conduct)
 
     for entry in strips_sent:
         wait_recv(entry)
@@ -549,7 +598,6 @@
 
     wait_face(0)
     faces_fine = face_planes([grown[0][p] for p in range(3 * planes)], True)
-    spread(0, coarse_conduct)
     wait_face(1)
     start = [grown[1][p] for p in range(3 * planes)]
     applied = operate_planes(faces_fine, start, 1, 3 * planes - 1)
@@ -560,6 +608,8 @@
     solved, residual = smooth_planes(faces_fine, residual, start, True)
     spread(
         1, restrict_fine([residual[planes + q][0:rows, 0:LANES] for q in range(planes)], 0.25))
+    settle_hop(0, True)
+    second_hop(0)
     for q in range(planes):
         out_fine[q] = solved[planes + q][0:rows, 0:LANES]
     stores[0].start()
@@ -573,7 +623,7 @@
         for from_x in range(count_x):
             blocks = [[], []]
             for from_z in range(count_z):
-                block = from_x * count_z + from_z
+                block = from_z * count_x + from_x
                 own = all_one[part, block]
                 low, high = all_half[part, 0, block], all_half[part, 1, block]
                 beside = jnp.concatenate(
@@ -632,6 +682,7 @@
     stores[4].start()
     for entry in strips_sent + [entry for _, entry in faces]:
         wait_send(entry)
+    settle_hop(0, False)
     settle(0, False)
     settle(1, False)
     for store in stores:
@@ -681,6 +732,7 @@
         pltpu.VMEM((3, FIELDS * planes // 2, ROWS, LANES), f32),
         pltpu.VMEM((2, rows // 2, LANES), f32),
         pltpu.VMEM((2, 2, ROWS, LANES), f32),
+        pltpu.VMEM((2, 2, count_x, ROWS, LANES), f32),
         pltpu.VMEM((2, blocks_all, rows // 2, LANES), f32),
         pltpu.VMEM((2, 2, blocks_all, ROWS, LANES), f32),
         pltpu.VMEM((rows, LANES), f32),
@@ -692,6 +744,7 @@
         dma((6,)), dma((6,)),
         dma((6,)), dma((6,)),
         dma((2, 3)), dma((2, 3)),
+        dma((2,)), dma((2,)),
         dma((5,)),
     ]
     outside = pl.BlockSpec(memory_space=pltpu.HBM)

time: 25.2 us -> 24.2 us (0.960)
  Pallas kernels: 24.3 us -> 23.4 us
    pallas_call x1, Pallas kernels: 22.8 us -> 21.8 us  [fused(): pl.pallas_call(functools.partial(kernel, sizes), out_shape=out_shape, in_...]
where the time goes in v4:
time: 24.2 us; the launch traced here: 24 us
  Pallas kernels  23.4 us (97%)
  between operations  0.64 us (3%)
    pallas_call x1, Pallas kernels, fused(): pl.pallas_call(functools.partial(kernel, sizes), out_shape=out_shape, in_...  21.8 us
    pallas_call x1, Pallas kernels, fused(): pl.pallas_call(hand_over, out_shape=out_shape, in_specs=[pl.BlockSpec(mem...  1.55 us

profile of v4, /device:TPU:0, one launch (start us, length us, event | category | flops | bytes accessed | tf_op | source)
XLA Modules:
  0.0 24.0 jit_solution(9237722108506199270)
XLA Ops:
  0.6 21.8 %shard_map.74 = (f32[4,32,128]{2,1,0:T(8,128)}, f32[2,16,64]{2,1,0:T(8,128)}, f32[4,8,32]{2,1,0:T(8,128)}, f32[2,4,16]{2,1,0:T(4,128)}, f32[2,4,16]{2,1,0:T(4,128)}) custom-call(f32[4,32,128]{2,1,0:T(8,128)} %refs_0_.1, f32[4,32,128]{2,1,0:T(8,128)} %refs_1_.1, f32[4,32,128]{2,1,0:T(8,128)} %refs_2_.1), custom_call_target="tpu_custom_call" | custom-call | tf_op jit(solution)/shard_map/pallas_call | solution.py:752
  22.5 1.5 %shard_map.75 = (f32[4,32,128]{2,1,0:T(8,128)}, f32[2,16,64]{2,1,0:T(8,128)}, f32[4,8,32]{2,1,0:T(8,128)}, f32[2,4,16]{2,1,0:T(4,128)}, f32[2,4,16]{2,1,0:T(4,128)}) custom-call(f32[4,32,128]{2,1,0:T(8,128)} %get-tuple-element.10.refs_0_, f32[2,16,64]{2,1,0:T(8,128)} %get-tuple-element.11.refs_1_, f32[4,8,32]{2,1,0:T(8,128)} %get-tuple-element.12.refs_2_, ...), custom_call_target="tpu_custom_call" | custom-call | tf_op jit(solution)/shard_map/pallas_call | solution.py:761

commit v5 on v4

--- a/solution.py
+++ b/solution.py
@@ -291,7 +291,7 @@
     inputs = refs[0:3]
     outs = refs[3:8]
     grown = refs[8:11]
-    (pack_full, pack_edge, pack_rows, got_full, got_edge, got_rows, own_one, own_half, line_half, all_one,
+    (pack_full, pack_edge, pack_rows, got_full, got_edge, got_rows, own_one, line_half, all_one,
      all_half, hold, solved_one, out_fine, out_one, out_two,
      out_three, out_rest, load_sem, face_send, face_recv, row_send, row_recv,
      full_send, full_recv, edge_send, edge_recv, one_send, one_recv, hop_send, hop_recv, store_sem) = refs[11:]
@@ -320,22 +320,23 @@
         [(f, q) for f in range(FIELDS) for q in range(planes)
          if q < WIDTH - 1 - (1 if f == 2 else 0)],
     ]
-    partners = [
-        (step, turn, dy)
-        for step in range(count_x)
-        for turn in range(count_z)
-        for dy in (0, -1, 1)
-        if (step, turn, dy) != (0, 0, 0)
-    ]
     barrier = pltpu.get_barrier_semaphore()
-    for dy in (0, -1, 1):
-        @pl.when(in_range(y + dy, count_y))
-        def _():
-            chosen = [p for p in partners if p[2] == dy]
-            for step, turn, _dy in chosen:
-                pl.semaphore_signal(
-                    barrier, inc=1, device_id=other(step, turn, dy),
-                    device_id_type=pl.DeviceIdType.MESH)
+
+    def greet(dx, dy, dz):
+        pl.semaphore_signal(
+            barrier, inc=1, device_id={"gx": x + dx, "gy": y + dy, "gz": lax.rem(z + dz, count_z)},
+            device_id_type=pl.DeviceIdType.MESH)
+
+    for dx in (0, 1, -1):
+        for dy in (0, 1, -1):
+            @pl.when(in_range(x + dx, count_x) & in_range(y + dy, count_y))
+            def _():
+                for dz in range(count_z):
+                    if (dx, dy, dz) != (0, 0, 0):
+                        greet(dx, dy, dz)
+    for distance in range(2, count_x):
+        for dx in (distance, -distance):
+            pl.when(in_range(x + dx, count_x))(functools.partial(greet, dx, 0, 0))
 
     for f in range(FIELDS):
         @pl.when(x == 0)
@@ -394,8 +395,9 @@
     pack_full[1] = jnp.where(low_lane, top, shift(bottom, WIDTH, 1))
     pack_edge[...] = jnp.where(first_z, packed[rows - ROWS :], packed[0:ROWS])
 
-    wanted = (count_x * count_z - 1) + count_x * count_z * (
-        jnp.where(y > 0, 1, 0) + jnp.where(y < count_y - 1, 1, 0))
+    beside_x = jnp.where(x > 0, 1, 0) + jnp.where(x < count_x - 1, 1, 0)
+    beside_y = jnp.where(y > 0, 1, 0) + jnp.where(y < count_y - 1, 1, 0)
+    wanted = (1 + beside_x) * (1 + beside_y) * count_z - 1 + (count_x - 1 - beside_x)
     pl.semaphore_wait(barrier, wanted)
 
     def send(src, dst, send_sem, recv_sem, device, to, back):
@@ -468,35 +470,8 @@
         pairs = [pair_rows(blocks[2 * q] + blocks[2 * q + 1], hold) for q in range(planes // 2)]
         return scale * split_dot(jnp.concatenate(pairs, axis=1), matrix_one)
 
-    hopped = (0,)
     here = z * count_x + x
     line = pl.ds(z * count_x, count_x)
-    blocks_all = count_x * count_z
-
-    def spread(part, value):
-        own_one[part] = value
-        top, bottom = value[0:ROWS], value[ROWS : 2 * ROWS]
-        own_half[part, 0] = jnp.where(quarter, shift(bottom, -(LANES // 4), 1), top)
-        own_half[part, 1] = jnp.where(quarter, top, shift(bottom, LANES // 4, 1))
-        all_one[part, here] = value
-        for dy in (0, 1, -1):
-            side = (1 - dy) // 2
-
-            def start():
-                for step, turn, _dy in [p for p in partners if p[2] == dy]:
-                    if dy == 0:
-                        source, target = own_one.at[part], all_one.at[part, here]
-                    else:
-                        source, target = own_half.at[part, side], all_half.at[part, side, here]
-                    pltpu.make_async_remote_copy(
-                        src_ref=source, dst_ref=target, send_sem=one_send.at[part, dy + 1],
-                        recv_sem=one_recv.at[part, dy + 1], device_id=other(step, turn, dy),
-                        device_id_type=pl.DeviceIdType.MESH).start()
-
-            if dy == 0:
-                start()
-            else:
-                pl.when(in_range(y + dy, count_y))(start)
 
     def remote(source, target, send_sem, recv_sem, device):
         return pltpu.make_async_remote_copy(
@@ -546,8 +521,7 @@
         for dy in (0, 1, -1):
             side = (1 - dy) // 2
             if dy == 0:
-                extent = count_x if part in hopped else blocks_all - 1
-                bytes_of = all_one.at[part, 0:extent]
+                bytes_of = all_one.at[part, line]
             else:
                 bytes_of = all_half.at[part, side]
             copy = remote(bytes_of, bytes_of, one_send.at[part, dy + 1],
@@ -606,10 +580,12 @@
     for p in range(1, 3 * planes - 1):
         residual[p] = grown[2][p] - applied[p]
     solved, residual = smooth_planes(faces_fine, residual, start, True)
-    spread(
+    first_hop(
         1, restrict_fine([residual[planes + q][0:rows, 0:LANES] for q in range(planes)], 0.25))
     settle_hop(0, True)
     second_hop(0)
+    settle_hop(1, True)
+    second_hop(1)
     for q in range(planes):
         out_fine[q] = solved[planes + q][0:rows, 0:LANES]
     stores[0].start()
@@ -683,6 +659,7 @@
     for entry in strips_sent + [entry for _, entry in faces]:
         wait_send(entry)
     settle_hop(0, False)
+    settle_hop(1, False)
     settle(0, False)
     settle(1, False)
     for store in stores:
@@ -731,7 +708,6 @@
         pltpu.VMEM((3, 2, ROWS, LANES), f32),
         pltpu.VMEM((3, FIELDS * planes // 2, ROWS, LANES), f32),
         pltpu.VMEM((2, rows // 2, LANES), f32),
-        pltpu.VMEM((2, 2, ROWS, LANES), f32),
         pltpu.VMEM((2, 2, count_x, ROWS, LANES), f32),
         pltpu.VMEM((2, blocks_all, rows // 2, LANES), f32),
         pltpu.VMEM((2, 2, blocks_all, ROWS, LANES), f32),

time: 24.2 us -> 24.8 us (1.025)
  Pallas kernels: 23.4 us -> 23.9 us
    pallas_call x1, Pallas kernels: 21.8 us -> 22.4 us  [fused(): pl.pallas_call(functools.partial(kernel, sizes), out_shape=out_shape, in_...]
where the time goes in v5:
time: 24.8 us; the launch traced here: 24.6 us
  Pallas kernels  23.9 us (96%)
  between operations  0.64 us (3%)
    pallas_call x1, Pallas kernels, fused(): pl.pallas_call(functools.partial(kernel, sizes), out_shape=out_shape, in_...  22.4 us
    pallas_call x1, Pallas kernels, fused(): pl.pallas_call(hand_over, out_shape=out_shape, in_specs=[pl.BlockSpec(mem...  1.55 us

profile of v5, /device:TPU:0, one launch (start us, length us, event | category | flops | bytes accessed | tf_op | source)
XLA Modules:
  0.0 24.6 jit_solution(17152446543584902486)
XLA Ops:
  0.6 22.4 %shard_map.74 = (f32[4,32,128]{2,1,0:T(8,128)}, f32[2,16,64]{2,1,0:T(8,128)}, f32[4,8,32]{2,1,0:T(8,128)}, f32[2,4,16]{2,1,0:T(4,128)}, f32[2,4,16]{2,1,0:T(4,128)}) custom-call(f32[4,32,128]{2,1,0:T(8,128)} %refs_0_.1, f32[4,32,128]{2,1,0:T(8,128)} %refs_1_.1, f32[4,32,128]{2,1,0:T(8,128)} %refs_2_.1), custom_call_target="tpu_custom_call" | custom-call | tf_op jit(solution)/shard_map/pallas_call | solution.py:728
  23.0 1.5 %shard_map.75 = (f32[4,32,128]{2,1,0:T(8,128)}, f32[2,16,64]{2,1,0:T(8,128)}, f32[4,8,32]{2,1,0:T(8,128)}, f32[2,4,16]{2,1,0:T(4,128)}, f32[2,4,16]{2,1,0:T(4,128)}) custom-call(f32[4,32,128]{2,1,0:T(8,128)} %get-tuple-element.10.refs_0_, f32[2,16,64]{2,1,0:T(8,128)} %get-tuple-element.11.refs_1_, f32[4,8,32]{2,1,0:T(8,128)} %get-tuple-element.12.refs_2_, ...), custom_call_target="tpu_custom_call" | custom-call | tf_op jit(solution)/shard_map/pallas_call | solution.py:737

commit v6 on v4

--- a/solution.py
+++ b/solution.py
@@ -367,6 +367,52 @@
             for part in range(2):
                 all_half[part, side] = jnp.zeros(all_half.shape[2:], jnp.float32)
 
+    wanted = (count_x * count_z - 1) + count_x * count_z * (
+        jnp.where(y > 0, 1, 0) + jnp.where(y < count_y - 1, 1, 0))
+    pl.semaphore_wait(barrier, wanted)
+
+    def send(src, dst, send_sem, recv_sem, device, to, back):
+        copy = pltpu.make_async_remote_copy(
+            src_ref=src, dst_ref=dst, send_sem=send_sem, recv_sem=recv_sem,
+            device_id=device, device_id_type=pl.DeviceIdType.MESH)
+        if to is None:
+            copy.start()
+        else:
+            pl.when(to)(copy.start)
+        return copy, to, back
+
+    def wait_recv(entry):
+        copy, _, back = entry
+        if back is None:
+            copy.wait_recv()
+        else:
+            pl.when(back)(copy.wait_recv)
+
+    def wait_send(entry):
+        copy, to, _ = entry
+        if to is None:
+            copy.wait_send()
+        else:
+            pl.when(to)(copy.wait_send)
+
+    faces = []
+    strips_sent = []
+
+    def send_face(f):
+        for dx in (1, -1):
+            to, back = in_range(x + dx, count_x), in_range(x - dx, count_x)
+            low, high = 0, planes
+            if f == 2:
+                low, high = (1, planes) if dx == 1 else (0, planes - 1)
+            base = 0 if dx == 1 else 2 * planes
+            index = (dx + 1) // 2 * FIELDS + f
+            faces.append((f, send(
+                inputs[f].at[low:high],
+                grown[f].at[base + low : base + high, 0:rows, 0:LANES],
+                face_send.at[index], face_recv.at[index],
+                {"gx": x + dx, "gy": y, "gz": z}, to, back)))
+
+    send_face(0)
     for load in loads:
         load.wait()
 
@@ -394,52 +440,6 @@
     pack_full[1] = jnp.where(low_lane, top, shift(bottom, WIDTH, 1))
     pack_edge[...] = jnp.where(first_z, packed[rows - ROWS :], packed[0:ROWS])
 
-    wanted = (count_x * count_z - 1) + count_x * count_z * (
-        jnp.where(y > 0, 1, 0) + jnp.where(y < count_y - 1, 1, 0))
-    pl.semaphore_wait(barrier, wanted)
-
-    def send(src, dst, send_sem, recv_sem, device, to, back):
-        copy = pltpu.make_async_remote_copy(
-            src_ref=src, dst_ref=dst, send_sem=send_sem, recv_sem=recv_sem,
-            device_id=device, device_id_type=pl.DeviceIdType.MESH)
-        if to is None:
-            copy.start()
-        else:
-            pl.when(to)(copy.start)
-        return copy, to, back
-
-    def wait_recv(entry):
-        copy, _, back = entry
-        if back is None:
-            copy.wait_recv()
-        else:
-            pl.when(back)(copy.wait_recv)
-
-    def wait_send(entry):
-        copy, to, _ = entry
-        if to is None:
-            copy.wait_send()
-        else:
-            pl.when(to)(copy.wait_send)
-
-    faces = []
-    strips_sent = []
-
-    def send_face(f):
-        for dx in (1, -1):
-            to, back = in_range(x + dx, count_x), in_range(x - dx, count_x)
-            low, high = 0, planes
-            if f == 2:
-                low, high = (1, planes) if dx == 1 else (0, planes - 1)
-            base = 0 if dx == 1 else 2 * planes
-            index = (dx + 1) // 2 * FIELDS + f
-            faces.append((f, send(
-                grown[f].at[planes + low : planes + high, 0:rows, 0:LANES],
-                grown[f].at[base + low : base + high, 0:rows, 0:LANES],
-                face_send.at[index], face_recv.at[index],
-                {"gx": x + dx, "gy": y, "gz": z}, to, back)))
-
-    send_face(0)
     for dx in (1, -1, 0):
         slot = 1 - dx
         to, back = (in_range(x + dx, count_x), in_range(x - dx, count_x)) if dx else (None, None)

time: 24.2 us -> 24.4 us (level)
  no operation moved by 1% of the time
where the time goes in v6:
time: 24.4 us; the launch traced here: 24.2 us
  Pallas kernels  23.6 us (97%)
  between operations  0.64 us (3%)
    pallas_call x1, Pallas kernels, fused(): pl.pallas_call(functools.partial(kernel, sizes), out_shape=out_shape, in_...  22 us
    pallas_call x1, Pallas kernels, fused(): pl.pallas_call(hand_over, out_shape=out_shape, in_specs=[pl.BlockSpec(mem...  1.55 us

profile of v6, /device:TPU:0, one launch (start us, length us, event | category | flops | bytes accessed | tf_op | source)
XLA Modules:
  0.0 24.2 jit_solution(10936590628830238494)
XLA Ops:
  0.6 22.0 %shard_map.74 = (f32[4,32,128]{2,1,0:T(8,128)}, f32[2,16,64]{2,1,0:T(8,128)}, f32[4,8,32]{2,1,0:T(8,128)}, f32[2,4,16]{2,1,0:T(4,128)}, f32[2,4,16]{2,1,0:T(4,128)}) custom-call(f32[4,32,128]{2,1,0:T(8,128)} %refs_0_.1, f32[4,32,128]{2,1,0:T(8,128)} %refs_1_.1, f32[4,32,128]{2,1,0:T(8,128)} %refs_2_.1), custom_call_target="tpu_custom_call" | custom-call | tf_op jit(solution)/shard_map/pallas_call | solution.py:752
  22.7 1.5 %shard_map.75 = (f32[4,32,128]{2,1,0:T(8,128)}, f32[2,16,64]{2,1,0:T(8,128)}, f32[4,8,32]{2,1,0:T(8,128)}, f32[2,4,16]{2,1,0:T(4,128)}, f32[2,4,16]{2,1,0:T(4,128)}) custom-call(f32[4,32,128]{2,1,0:T(8,128)} %get-tuple-element.10.refs_0_, f32[2,16,64]{2,1,0:T(8,128)} %get-tuple-element.11.refs_1_, f32[4,8,32]{2,1,0:T(8,128)} %get-tuple-element.12.refs_2_, ...), custom_call_target="tpu_custom_call" | custom-call | tf_op jit(solution)/shard_map/pallas_call | solution.py:761

commit v7 on v4

--- a/solution.py
+++ b/solution.py
@@ -226,6 +226,48 @@
     return result
 
 
+def coarse_faces(conduct):
+    count, length = len(conduct), conduct[0].shape[0]
+    row = lax.broadcasted_iota(jnp.int32, conduct[0].shape, 0)
+    first, last = row == 0, row == length - 1
+    weights, diagonals, inverses = [], [], []
+    for i in range(count):
+        own = conduct[i]
+        half = 0.5 * own
+        below = 0.5 * (own + conduct[i - 1]) if i > 0 else half
+        above = 0.5 * (own + conduct[i + 1]) if i + 1 < count else half
+        before = jnp.where(first, half, 0.5 * (own + shift(own, 1, 0)))
+        after = jnp.where(last, half, 0.5 * (own + shift(own, -1, 0)))
+        left = 0.5 * (own + shift(own, 1, 1))
+        right = 0.5 * (own + shift(own, -1, 1))
+        diagonal = (below + above) + (before + after) + (left + right)
+        inside = own > 0.0
+        diagonals.append(diagonal)
+        inverses.append(jnp.where(inside, 1.0 / jnp.where(inside, diagonal, 1.0), 0.0))
+        before = jnp.where(first, 0.0, before)
+        after = jnp.where(last, 0.0, after)
+        weights.append((below, above, before, after, left, right))
+    return weights, diagonals, None, inverses
+
+
+def operate_coarse(faces, field):
+    weights, diagonals = faces[0], faces[1]
+    count = len(field)
+    result = []
+    for i in range(count):
+        below, above, before, after, left, right = weights[i]
+        own = field[i]
+        value = diagonals[i] * own
+        if i > 0:
+            value = value - below * field[i - 1]
+        if i + 1 < count:
+            value = value - above * field[i + 1]
+        rolled = before * shift(own, 1, 0) + after * shift(own, -1, 0)
+        rolled = rolled + (left * shift(own, 1, 1) + right * shift(own, -1, 1))
+        result.append(value - rolled)
+    return result
+
+
 def smooth_planes(faces, residual, start, grown):
     theta = 0.5 * (upper_bound + lower_bound)
     delta = 0.5 * (upper_bound - lower_bound)
@@ -244,7 +286,10 @@
         for i in range(low, high):
             solution[i] = direction[i] if solution[i] is None else solution[i] + direction[i]
         low, high = low + edge, high - edge
-        applied = operate_planes(faces, direction, low, high)
+        if grown:
+            applied = operate_planes(faces, direction, low, high)
+        else:
+            applied = operate_coarse(faces, direction)
         for i in range(low, high):
             residual[i] = residual[i] - applied[i]
         if sweep_index + 1 < SWEEPS:
@@ -275,15 +320,16 @@
 def pair_matrix(keep_low, keep_high, offset):
     source = lax.broadcasted_iota(jnp.int32, (LANES, LANES), 0)
     target = lax.broadcasted_iota(jnp.int32, (LANES, LANES), 1)
-    low = (source < keep_low) & (target == offset + source // 2)
-    high = (source >= LANES - keep_high) & (target == LANES // 2 + source // 2)
+    low = (source < keep_low) & (target == offset + (source >> 1))
+    high = (source >= LANES - keep_high) & (target == LANES // 2 + (source >> 1))
     return jnp.where(low | high, 1.0, 0.0).astype(jnp.bfloat16)
 
 
-def pair_rows(value, hold):
+def pair_rows(value, hold, q):
     rows = value.shape[0]
-    hold[0:rows, :] = value
-    return hold[pl.ds(0, rows // 2, stride=2), :] + hold[pl.ds(1, rows // 2, stride=2), :]
+    hold[q, 0:rows, :] = value
+    even = hold[q, pl.ds(0, rows // 2, stride=2), :]
+    return even + hold[q, pl.ds(1, rows // 2, stride=2), :]
 
 
 def kernel(sizes, *refs):
@@ -372,7 +418,7 @@
 
     lane = lax.broadcasted_iota(jnp.int32, (rows, LANES), 1)
     row_index = lax.broadcasted_iota(jnp.int32, (ROWS, LANES), 0)
-    low_lane = lax.rem(lane[0 : rows // 2], 2 * WIDTH) < WIDTH
+    low_lane = (lane[0 : rows // 2] & WIDTH) == 0
     leave = (row_index < WIDTH) == jnp.logical_not(first_z)
     strips = {}
     packed = jnp.zeros((rows, LANES), jnp.float32)
@@ -382,7 +428,7 @@
             piece = grown[f][planes + q, 0:rows, 0:LANES]
             strips[f, q] = jnp.where(first_z, piece[rows - ROWS :], piece[0:ROWS])
             moved = shift(piece, 2 * WIDTH * k, 1)
-            window = lax.rem(lane - 2 * WIDTH * k + WIDTH + LANES, LANES) < 2 * WIDTH
+            window = ((lane + (LANES + WIDTH - 2 * WIDTH * k)) & (LANES - 1)) < 2 * WIDTH
             packed = jnp.where(window, moved, packed)
     for slot in range(3):
         for t in range(len(strip_list[slot]) // 2):
@@ -462,10 +508,10 @@
 
     to_one = [pair_matrix(LANES, 0, 0), pair_matrix(LANES, 0, LANES // 2)]
     matrix_one = jnp.concatenate(to_one, axis=0)
-    quarter = lax.broadcasted_iota(jnp.int32, (ROWS, LANES), 1) % (LANES // 2) < LANES // 4
+    quarter = (lax.broadcasted_iota(jnp.int32, (ROWS, LANES), 1) & (LANES // 4)) == 0
 
     def restrict_fine(blocks, scale):
-        pairs = [pair_rows(blocks[2 * q] + blocks[2 * q + 1], hold) for q in range(planes // 2)]
+        pairs = [pair_rows(blocks[2 * q] + blocks[2 * q + 1], hold, q) for q in range(planes // 2)]
         return scale * split_dot(jnp.concatenate(pairs, axis=1), matrix_one)
 
     hopped = (0,)
@@ -616,7 +662,6 @@
 
     lane_one = lax.broadcasted_iota(jnp.int32, (2 * ROWS, LANES), 1)
     lower = lane_one < LANES // 2
-    empty = jnp.zeros((ROWS, LANES), jnp.float32)
 
     def assemble(part):
         level = []
@@ -633,21 +678,18 @@
                 blocks[0].append(jnp.where(lower, own, shift(beside, LANES // 2, 1)))
                 blocks[1].append(jnp.where(lower, shift(own, LANES // 2, 1), beside))
             for q in range(2):
-                level.append(jnp.concatenate(blocks[q] + [empty], axis=0))
+                level.append(jnp.concatenate(blocks[q], axis=0))
         return level
 
     def restrict(level, matrix, scale):
-        length = level[0].shape[0] - ROWS
+        length = level[0].shape[0]
         summed = []
         for q in range(len(level) // 2):
             both = level[2 * q] + level[2 * q + 1]
-            summed.append(pair_rows(both[0:length], hold))
+            summed.append(pair_rows(both, hold, q))
         joined = scale * split_dot(jnp.concatenate(summed, axis=0), matrix)
         half = length // 2
-        return [
-            jnp.concatenate([joined[q * half : (q + 1) * half], empty], axis=0)
-            for q in range(len(summed))
-        ]
+        return [joined[q * half : (q + 1) * half] for q in range(len(summed))]
 
     matrix_two = pair_matrix(3 * LANES // 4, LANES // 4, 0)
     matrix_three = pair_matrix(3 * LANES // 8, LANES // 8, 0)
@@ -656,7 +698,7 @@
     conduct_two = restrict(conduct_one, matrix_two, 0.125)
     conduct_three = restrict(conduct_two, matrix_three, 0.125)
     faces_one, faces_two, faces_three = (
-        face_planes(conduct, False) for conduct in (conduct_one, conduct_two, conduct_three))
+        coarse_faces(conduct) for conduct in (conduct_one, conduct_two, conduct_three))
 
     settle(1, True)
     solved, residual = smooth_planes(faces_one, assemble(1), None, False)
@@ -735,7 +777,7 @@
         pltpu.VMEM((2, 2, count_x, ROWS, LANES), f32),
         pltpu.VMEM((2, blocks_all, rows // 2, LANES), f32),
         pltpu.VMEM((2, 2, blocks_all, ROWS, LANES), f32),
-        pltpu.VMEM((rows, LANES), f32),
+        pltpu.VMEM((count_x, rows, LANES), f32),
         pltpu.VMEM((2 * count_x, rows // 2, LANES), f32),
         *[pltpu.VMEM(shape, f32) for shape in shapes],
         dma((3,)),

time: 24.2 us -> 23.7 us (0.979)
  Pallas kernels: 23.4 us -> 22.8 us
    pallas_call x1, Pallas kernels: 21.8 us -> 21.3 us  [fused(): pl.pallas_call(functools.partial(kernel, sizes), out_shape=out_shape, in_...]
where the time goes in v7:
time: 23.7 us; the launch traced here: 23.5 us
  Pallas kernels  22.8 us (96%)
  between operations  0.64 us (3%)
    pallas_call x1, Pallas kernels, fused(): pl.pallas_call(functools.partial(kernel, sizes), out_shape=out_shape, in_...  21.3 us
    pallas_call x1, Pallas kernels, fused(): pl.pallas_call(hand_over, out_shape=out_shape, in_specs=[pl.BlockSpec(mem...  1.55 us

profile of v7, /device:TPU:0, one launch (start us, length us, event | category | flops | bytes accessed | tf_op | source)
XLA Modules:
  0.0 23.5 jit_solution(9133009868820625096)
XLA Ops:
  0.6 21.3 %shard_map.74 = (f32[4,32,128]{2,1,0:T(8,128)}, f32[2,16,64]{2,1,0:T(8,128)}, f32[4,8,32]{2,1,0:T(8,128)}, f32[2,4,16]{2,1,0:T(4,128)}, f32[2,4,16]{2,1,0:T(4,128)}) custom-call(f32[4,32,128]{2,1,0:T(8,128)} %refs_0_.1, f32[4,32,128]{2,1,0:T(8,128)} %refs_1_.1, f32[4,32,128]{2,1,0:T(8,128)} %refs_2_.1), custom_call_target="tpu_custom_call" | custom-call | tf_op jit(solution)/shard_map/pallas_call | solution.py:794
  21.9 1.5 %shard_map.75 = (f32[4,32,128]{2,1,0:T(8,128)}, f32[2,16,64]{2,1,0:T(8,128)}, f32[4,8,32]{2,1,0:T(8,128)}, f32[2,4,16]{2,1,0:T(4,128)}, f32[2,4,16]{2,1,0:T(4,128)}) custom-call(f32[4,32,128]{2,1,0:T(8,128)} %get-tuple-element.10.refs_0_, f32[2,16,64]{2,1,0:T(8,128)} %get-tuple-element.11.refs_1_, f32[4,8,32]{2,1,0:T(8,128)} %get-tuple-element.12.refs_2_, ...), custom_call_target="tpu_custom_call" | custom-call | tf_op jit(solution)/shard_map/pallas_call | solution.py:803

commit v8 on v7

--- a/solution.py
+++ b/solution.py
@@ -268,7 +268,7 @@
     return result
 
 
-def smooth_planes(faces, residual, start, grown):
+def smooth_planes(faces, residual, start, grown, between=None):
     theta = 0.5 * (upper_bound + lower_bound)
     delta = 0.5 * (upper_bound - lower_bound)
     sigma = theta / delta
@@ -292,6 +292,8 @@
             applied = operate_coarse(faces, direction)
         for i in range(low, high):
             residual[i] = residual[i] - applied[i]
+        if between is not None and sweep_index == 0:
+            between()
         if sweep_index + 1 < SWEEPS:
             ratio_next = 1.0 / (2.0 * sigma - ratio_now)
             turned = [None] * count
@@ -368,7 +370,7 @@
     ]
     partners = [
         (step, turn, dy)
-        for step in range(count_x)
+        for step in sorted(range(count_x), key=lambda step: -min(step, count_x - step))
         for turn in range(count_z)
         for dy in (0, -1, 1)
         if (step, turn, dy) != (0, 0, 0)
@@ -651,11 +653,14 @@
     residual = [None] * (3 * planes)
     for p in range(1, 3 * planes - 1):
         residual[p] = grown[2][p] - applied[p]
-    solved, residual = smooth_planes(faces_fine, residual, start, True)
+
+    def pass_on():
+        settle_hop(0, True)
+        second_hop(0)
+
+    solved, residual = smooth_planes(faces_fine, residual, start, True, pass_on)
     spread(
         1, restrict_fine([residual[planes + q][0:rows, 0:LANES] for q in range(planes)], 0.25))
-    settle_hop(0, True)
-    second_hop(0)
     for q in range(planes):
         out_fine[q] = solved[planes + q][0:rows, 0:LANES]
     stores[0].start()

time: 23.7 us -> 24.4 us (1.030)
  Pallas kernels: 22.8 us -> 23.4 us
    pallas_call x1, Pallas kernels: 21.3 us -> 21.9 us  [fused(): pl.pallas_call(functools.partial(kernel, sizes), out_shape=out_shape, in_...]
where the time goes in v8:
time: 24.4 us; the launch traced here: 24.1 us
  Pallas kernels  23.4 us (96%)
  between operations  0.64 us (3%)
    pallas_call x1, Pallas kernels, fused(): pl.pallas_call(functools.partial(kernel, sizes), out_shape=out_shape, in_...  21.9 us
    pallas_call x1, Pallas kernels, fused(): pl.pallas_call(hand_over, out_shape=out_shape, in_specs=[pl.BlockSpec(mem...  1.55 us

profile of v8, /device:TPU:0, one launch (start us, length us, event | category | flops | bytes accessed | tf_op | source)
XLA Modules:
  0.0 24.1 jit_solution(17984964573109117503)
XLA Ops:
  0.6 21.9 %shard_map.74 = (f32[4,32,128]{2,1,0:T(8,128)}, f32[2,16,64]{2,1,0:T(8,128)}, f32[4,8,32]{2,1,0:T(8,128)}, f32[2,4,16]{2,1,0:T(4,128)}, f32[2,4,16]{2,1,0:T(4,128)}) custom-call(f32[4,32,128]{2,1,0:T(8,128)} %refs_0_.1, f32[4,32,128]{2,1,0:T(8,128)} %refs_1_.1, f32[4,32,128]{2,1,0:T(8,128)} %refs_2_.1), custom_call_target="tpu_custom_call" | custom-call | tf_op jit(solution)/shard_map/pallas_call | solution.py:799
  22.5 1.5 %shard_map.75 = (f32[4,32,128]{2,1,0:T(8,128)}, f32[2,16,64]{2,1,0:T(8,128)}, f32[4,8,32]{2,1,0:T(8,128)}, f32[2,4,16]{2,1,0:T(4,128)}, f32[2,4,16]{2,1,0:T(4,128)}) custom-call(f32[4,32,128]{2,1,0:T(8,128)} %get-tuple-element.10.refs_0_, f32[2,16,64]{2,1,0:T(8,128)} %get-tuple-element.11.refs_1_, f32[4,8,32]{2,1,0:T(8,128)} %get-tuple-element.12.refs_2_, ...), custom_call_target="tpu_custom_call" | custom-call | tf_op jit(solution)/shard_map/pallas_call | solution.py:808

commit v9 on v7

--- a/solution.py
+++ b/solution.py
@@ -203,7 +203,7 @@
     return weight_x, weight_y, weight_z, inverse
 
 
-def operate_planes(faces, field, low, high):
+def operate_planes(faces, field, low, high, keep=None):
     weight_x, weight_y, weight_z, _ = faces
     count = len(field)
     flux_x = [None] * (count + 1)
@@ -215,13 +215,15 @@
         else:
             flux_x[i] = weight_x[i] * (field[i] - field[i - 1])
     result = [None] * count
+    rows, lanes = keep if keep is not None else field[low].shape
     for i in range(low, high):
         flux_z = weight_z[i] * (field[i] - shift(field[i], -1, 0))
         flux_y = weight_y[i] * (field[i] - shift(field[i], -1, 1))
+        flux_z, flux_y = flux_z[:, 0:lanes], flux_y[0:rows]
         result[i] = (
-            (flux_x[i] - flux_x[i + 1])
-            + (flux_z - shift(flux_z, 1, 0))
-            + (flux_y - shift(flux_y, 1, 1))
+            (flux_x[i] - flux_x[i + 1])[0:rows, 0:lanes]
+            + (flux_z - shift(flux_z, 1, 0))[0:rows]
+            + (flux_y - shift(flux_y, 1, 1))[:, 0:lanes]
         )
     return result
 
@@ -268,7 +270,7 @@
     return result
 
 
-def smooth_planes(faces, residual, start, grown):
+def smooth_planes(faces, residual, start, grown, block=None):
     theta = 0.5 * (upper_bound + lower_bound)
     delta = 0.5 * (upper_bound - lower_bound)
     sigma = theta / delta
@@ -287,11 +289,13 @@
             solution[i] = direction[i] if solution[i] is None else solution[i] + direction[i]
         low, high = low + edge, high - edge
         if grown:
-            applied = operate_planes(faces, direction, low, high)
+            keep = block if sweep_index + 1 == SWEEPS else None
+            applied = operate_planes(faces, direction, low, high, keep)
         else:
             applied = operate_coarse(faces, direction)
         for i in range(low, high):
-            residual[i] = residual[i] - applied[i]
+            extent = applied[i].shape
+            residual[i] = residual[i][0 : extent[0], 0 : extent[1]] - applied[i]
         if sweep_index + 1 < SWEEPS:
             ratio_next = 1.0 / (2.0 * sigma - ratio_now)
             turned = [None] * count
@@ -368,7 +372,7 @@
     ]
     partners = [
         (step, turn, dy)
-        for step in range(count_x)
+        for step in sorted(range(count_x), key=lambda step: -min(step, count_x - step))
         for turn in range(count_z)
         for dy in (0, -1, 1)
         if (step, turn, dy) != (0, 0, 0)
@@ -651,9 +655,10 @@
     residual = [None] * (3 * planes)
     for p in range(1, 3 * planes - 1):
         residual[p] = grown[2][p] - applied[p]
-    solved, residual = smooth_planes(faces_fine, residual, start, True)
+    solved, residual = smooth_planes(
+        faces_fine, residual, start, True, (rows, LANES))
     spread(
-        1, restrict_fine([residual[planes + q][0:rows, 0:LANES] for q in range(planes)], 0.25))
+        1, restrict_fine([residual[planes + q] for q in range(planes)], 0.25))
     settle_hop(0, True)
     second_hop(0)
     for q in range(planes):

time: 23.7 us -> 23.6 us (level)
  no operation moved by 1% of the time
where the time goes in v9:
time: 23.6 us; the launch traced here: 23.4 us
  Pallas kernels  22.8 us (97%)
  between operations  0.64 us (3%)
    pallas_call x1, Pallas kernels, fused(): pl.pallas_call(functools.partial(kernel, sizes), out_shape=out_shape, in_...  21.2 us
    pallas_call x1, Pallas kernels, fused(): pl.pallas_call(hand_over, out_shape=out_shape, in_specs=[pl.BlockSpec(mem...  1.55 us

profile of v9, /device:TPU:0, one launch (start us, length us, event | category | flops | bytes accessed | tf_op | source)
XLA Modules:
  0.0 23.4 jit_solution(4528791578805689011)
XLA Ops:
  0.6 21.2 %shard_map.74 = (f32[4,32,128]{2,1,0:T(8,128)}, f32[2,16,64]{2,1,0:T(8,128)}, f32[4,8,32]{2,1,0:T(8,128)}, f32[2,4,16]{2,1,0:T(4,128)}, f32[2,4,16]{2,1,0:T(4,128)}) custom-call(f32[4,32,128]{2,1,0:T(8,128)} %refs_0_.1, f32[4,32,128]{2,1,0:T(8,128)} %refs_1_.1, f32[4,32,128]{2,1,0:T(8,128)} %refs_2_.1), custom_call_target="tpu_custom_call" | custom-call | tf_op jit(solution)/shard_map/pallas_call | solution.py:799
  21.9 1.5 %shard_map.75 = (f32[4,32,128]{2,1,0:T(8,128)}, f32[2,16,64]{2,1,0:T(8,128)}, f32[4,8,32]{2,1,0:T(8,128)}, f32[2,4,16]{2,1,0:T(4,128)}, f32[2,4,16]{2,1,0:T(4,128)}) custom-call(f32[4,32,128]{2,1,0:T(8,128)} %get-tuple-element.10.refs_0_, f32[2,16,64]{2,1,0:T(8,128)} %get-tuple-element.11.refs_1_, f32[4,8,32]{2,1,0:T(8,128)} %get-tuple-element.12.refs_2_, ...), custom_call_target="tpu_custom_call" | custom-call | tf_op jit(solution)/shard_map/pallas_call | solution.py:808

commit v10 on v9

--- a/solution.py
+++ b/solution.py
@@ -489,7 +489,6 @@
                 face_send.at[index], face_recv.at[index],
                 {"gx": x + dx, "gy": y, "gz": z}, to, back)))
 
-    send_face(0)
     for dx in (1, -1, 0):
         slot = 1 - dx
         to, back = (in_range(x + dx, count_x), in_range(x - dx, count_x)) if dx else (None, None)
@@ -507,6 +506,7 @@
             strips_sent.append(send(
                 pack_edge, got_edge.at[slot, side], edge_send.at[slot * 2 + side],
                 edge_recv.at[slot * 2 + side], {"gx": x + dx, "gy": y + dy, "gz": 1 - z}, to, back))
+    send_face(0)
     send_face(1)
     send_face(2)
 

time: 23.6 us -> 23.2 us (0.983)
  Pallas kernels: 22.8 us -> 22.3 us
    pallas_call x1, Pallas kernels: 21.2 us -> 20.8 us  [fused(): pl.pallas_call(functools.partial(kernel, sizes), out_shape=out_shape, in_...]
where the time goes in v10:
time: 23.2 us; the launch traced here: 22.9 us
  Pallas kernels  22.3 us (96%)
  between operations  0.64 us (3%)
    pallas_call x1, Pallas kernels, fused(): pl.pallas_call(functools.partial(kernel, sizes), out_shape=out_shape, in_...  20.8 us
    pallas_call x1, Pallas kernels, fused(): pl.pallas_call(hand_over, out_shape=out_shape, in_specs=[pl.BlockSpec(mem...  1.55 us

profile of v10, /device:TPU:0, one launch (start us, length us, event | category | flops | bytes accessed | tf_op | source)
XLA Modules:
  0.0 22.9 jit_solution(17087487569036179727)
XLA Ops:
  0.6 20.8 %shard_map.74 = (f32[4,32,128]{2,1,0:T(8,128)}, f32[2,16,64]{2,1,0:T(8,128)}, f32[4,8,32]{2,1,0:T(8,128)}, f32[2,4,16]{2,1,0:T(4,128)}, f32[2,4,16]{2,1,0:T(4,128)}) custom-call(f32[4,32,128]{2,1,0:T(8,128)} %refs_0_.1, f32[4,32,128]{2,1,0:T(8,128)} %refs_1_.1, f32[4,32,128]{2,1,0:T(8,128)} %refs_2_.1), custom_call_target="tpu_custom_call" | custom-call | tf_op jit(solution)/shard_map/pallas_call | solution.py:799
  21.4 1.5 %shard_map.75 = (f32[4,32,128]{2,1,0:T(8,128)}, f32[2,16,64]{2,1,0:T(8,128)}, f32[4,8,32]{2,1,0:T(8,128)}, f32[2,4,16]{2,1,0:T(4,128)}, f32[2,4,16]{2,1,0:T(4,128)}) custom-call(f32[4,32,128]{2,1,0:T(8,128)} %get-tuple-element.10.refs_0_, f32[2,16,64]{2,1,0:T(8,128)} %get-tuple-element.11.refs_1_, f32[4,8,32]{2,1,0:T(8,128)} %get-tuple-element.12.refs_2_, ...), custom_call_target="tpu_custom_call" | custom-call | tf_op jit(solution)/shard_map/pallas_call | solution.py:808
